TPU v7x, 512 devices: a whole 4x4x16 slice. The times are simulated.
512 devices in a mesh: hid: 16 (over y, x), inter: 32 (over z, core).
Axes of the slice: x: 4, y: 4, z: 16, core: 2. Of those that a mesh axis runs over, the one named last changes fastest.
Arguments:
- tokens: bfloat16 [256, 16384], P('inter', 'hid'), may hold values from -6 to 6
- gate_words: float32 [4096, 40960], P('hid', 'inter'), may hold values from 0 to 65535, as said below
- gate_scales: bfloat16 [128, 40960], P('hid', 'inter'), may hold values from 0.00077819824 to 0.003112793
- gate_zeros: int32 [128, 40960], P('hid', 'inter'), may hold values from 7 to 9
- up_words: float32 [4096, 40960], P('hid', 'inter'), may hold values from 0 to 65535, as said below
- up_scales: bfloat16 [128, 40960], P('hid', 'inter'), may hold values from 0.00077819824 to 0.003112793
- up_zeros: int32 [128, 40960], P('hid', 'inter'), may hold values from 7 to 9
- sign_bits: int32 [40960], P('inter'), may hold values 0 or 1
- down_words: float32 [10240, 16384], P('inter', 'hid'), may hold values from 0 to 65535, as said below
- down_scales: bfloat16 [320, 16384], P('inter', 'hid'), may hold values from 0.00049209595 to 0.0019683838
- down_zeros: int32 [320, 16384], P('inter', 'hid'), may hold values from 7 to 9
Outputs:
- mixed: bfloat16 [256, 16384], P('inter', 'hid')
Inputs may be any that keep to these rules, and one draw needn't show every extreme that they name: `gate_words`: each word is a whole number holding four 4-bit codes, the k-th in the base-16 digit k. `up_words`: each word is a whole number holding four 4-bit codes, the k-th in the base-16 digit k. `down_words`: each word is a whole number holding four 4-bit codes, the k-th in the base-16 digit k.
All inputs are finite; a program needn't handle non-finite values. No bound on the sum of `sign_bits` on one device may be relied on, other than what follows from the above.
Results may differ from a plain program's by a relative error of at most 0.0067.
Values may be sent and summed in bfloat16 or wider, within the bound.
A program may use at most 64 MiB of HBM per device.

v0:
```python
import math

import jax
import jax.numpy as jnp
from jax import lax
from jax.sharding import PartitionSpec as P


def swapped(block, axis, distance):
    count = lax.axis_size(axis)
    route = []
    for low in range(count):
        high = low | 1 << distance
        if high != low and high < count:
            route += [(low, high), (high, low)]
    return lax.ppermute(block, axis, route)


def unpack_codes(packed):
    pieces = []
    for k in range(4):
        lower = jnp.floor(packed / float(16**k))
        higher = jnp.floor(packed / float(16 ** (k + 1)))
        pieces.append(lower - 16.0 * higher)
    return jnp.stack(pieces, axis=1).reshape(packed.shape[0] * 4, packed.shape[1])


def dequantize(packed, scales, zero_points):
    code_values = unpack_codes(packed)
    groups = code_values.shape[0] // 128
    grouped = code_values.reshape(groups, 128, code_values.shape[1])
    weight = (grouped - zero_points[:, None, :].astype(grouped.dtype)) * scales[:, None, :].astype(
        grouped.dtype
    )
    return weight.reshape(groups * 128, code_values.shape[1]).astype(jnp.bfloat16)


def sylvester(order):
    index_col = jnp.arange(order, dtype=jnp.int32)
    parity = jnp.zeros((order, order), jnp.int32)
    for bit_pos in range(order.bit_length() - 1):
        both = jnp.bitwise_and(
            jnp.right_shift(index_col[:, None], bit_pos),
            jnp.right_shift(index_col[None, :], bit_pos),
        )
        parity = parity + jnp.bitwise_and(both, 1)
    return (1 - 2 * jnp.bitwise_and(parity, 1)).astype(jnp.float32)


def body(
    tokens,
    gate_words,
    gate_scales,
    gate_zeros,
    up_words,
    up_scales,
    up_zeros,
    sign_bits,
    down_words,
    down_scales,
    down_zeros,
):
    gate_weight = dequantize(gate_words, gate_scales, gate_zeros)
    up_weight = dequantize(up_words, up_scales, up_zeros)
    local = gate_weight.shape[1]
    ranks = lax.axis_size("inter")
    piece = lax.all_gather(tokens, "inter", axis=0, tiled=True)
    partial_sums = jnp.concatenate(
        [
            jnp.dot(piece, gate_weight, preferred_element_type=jnp.float32),
            jnp.dot(piece, up_weight, preferred_element_type=jnp.float32),
        ],
        axis=1,
    )
    summed = lax.psum_scatter(partial_sums, "hid", scatter_dimension=0, tiled=True)
    hidden = jax.nn.silu(summed[:, :local]) * summed[:, local:]
    signed = hidden * (1 - 2 * sign_bits).astype(jnp.float32)[None, :]
    row_count = signed.shape[0]
    position = lax.axis_index("inter")
    across = signed
    for bit_pos in range(ranks.bit_length() - 1):
        partner = swapped(across, "inter", bit_pos)
        upper = jnp.bitwise_and(jnp.right_shift(position, bit_pos), 1) == 1
        across = jnp.where(upper, partner - across, across + partner)
    blocked = across.reshape(row_count, local // 128, 128)
    blocked = jnp.einsum("rbk,kl->rbl", blocked, sylvester(128), precision=lax.Precision.HIGHEST)
    rotated = (blocked.reshape(row_count, local) / math.sqrt(ranks * 128)).astype(jnp.bfloat16)
    full_rows = lax.all_gather(rotated, "hid", axis=0, tiled=True)
    down_weight = dequantize(down_words, down_scales, down_zeros)
    mixed = lax.psum_scatter(
        jnp.dot(full_rows, down_weight, preferred_element_type=jnp.float32),
        "inter",
        scatter_dimension=0,
        tiled=True,
    )
    return mixed.astype(jnp.bfloat16)


def solution(mesh):
    in_specs = (
        P("inter", "hid"),
        P("hid", "inter"),
        P("hid", "inter"),
        P("hid", "inter"),
        P("hid", "inter"),
        P("hid", "inter"),
        P("hid", "inter"),
        P("inter"),
        P("inter", "hid"),
        P("inter", "hid"),
        P("inter", "hid"),
    )
    out_specs = P("inter", "hid")
    return jax.shard_map(body, mesh=mesh, in_specs=in_specs, out_specs=out_specs, check_vma=False)
```

profile of v0, /device:TPU:1, one launch (start us, length us, event | category | flops | bytes accessed | tf_op | source)
XLA Modules:
  0.0 378.1 jit_solution(5541948337641090645)
XLA Ops:
  6.5 0.0 reduce-scatter.7.cloned.1.call-start
  6.5 2.0 subtract_bitcast_fusion.11
  8.6 0.4 pad_maximum_fusion
  9.0 5.8 %copy.45 = f32[256,4,1280]{2,1,0:T(4,128)} copy(f32[256,4,1280]{2,0,1:T(8,128)S(1)} %pad_maximum_fusion) | data formatting | bytes 10485760 | tf_op jit(solution)/shard_map/stack | solution.py:25
  14.8 7.4 %reshape_reshape.9 = f32[1024,1280]{1,0:T(8,128)} reshape(f32[256,4,1280]{2,1,0:T(4,128)} %copy.45) | data formatting | bytes 10485760 | tf_op jit(solution)/shard_map/reshape;reshape | solution.py:31
  22.2 0.0 copy-done.3
  22.2 0.0 copy-done.6
  22.2 0.0 copy-done.8
  22.2 39.2 %all_gather.6 = bf16[256,1024]{1,0:T(8,128)(2,1)S(1)} all-gather(bf16[8,1024]{1,0:T(8,128)(2,1)S(1)} %copy-done.8), channel_id=1, replica_groups=mesh['hid'=16,'inter'=32] {'inter'}, dimensions={0}, use_global_device_ids=true | all-gather | bytes 540672 | tf_op jit(solution)/shard_map/all_gather | solution.py:67
  61.4 0.7 subtract_bitcast_fusion.7
  62.1 0.4 pad_maximum_fusion.1
  62.6 5.7 %copy.46 = f32[256,4,1280]{2,1,0:T(4,128)} copy(f32[256,4,1280]{2,0,1:T(8,128)S(1)} %pad_maximum_fusion.1) | data formatting | bytes 10485760 | tf_op jit(solution)/shard_map/stack | solution.py:25
  68.3 7.3 %reshape_reshape.10 = f32[1024,1280]{1,0:T(8,128)} reshape(f32[256,4,1280]{2,1,0:T(4,128)} %copy.46) | data formatting | bytes 10485760 | tf_op jit(solution)/shard_map/reshape;reshape | solution.py:31
  75.5 0.0 copy-done.4
  75.6 0.0 slice-start.1
  75.6 3.2 fusion.2
  78.7 0.9 convolution_bitcast_fusion.1
  79.7 0.5 fusion.1
  80.2 0.9 convolution_bitcast_fusion
  81.1 0.2 pad_maximum_fusion.3
  81.3 2.1 copy.52
  83.4 0.0 reduce-scatter.7.cloned.1.call-update
  83.4 0.0 reduce-scatter.5.cloned.1.call-start
  83.5 0.6 copy-done.9
  84.1 3.7 subtract_bitcast_fusion.3
  87.8 80.1 %reduce-scatter.7.cloned.1.call-done = f32[16,2560]{1,0:T(8,128)} async-done(((f32[256,2560]{1,0:T(8,128)}), f32[16,2560]{1,0:T(8,128)}) %reduce-scatter.7.cloned.1.call-update) | async-done | bytes 163856 | tf_op jit(solution)/shard_map/reduce_scatter | solution.py:75
  167.9 1.0 fusion.7
  168.9 4.5 %collective-permute-start = (f32[16,1280]{1,0:T(8,128)S(1)}, f32[16,1280]{1,0:T(8,128)S(1)}, u32[]{:S(2)}, u32[]{:S(2)}) collective-permute-start(f32[16,1280]{1,0:T(8,128)S(1)} %fusion.7), channel_id=1, source_target_pairs={{0,1},{1,0},{2,3},{3,2},{4,5},{5,4},{6,7},{7,6},{8,9},{9,8},{10,11... | collective-permute-start | bytes 245768 | tf_op jit(solution)/shard_map/ppermute | solution.py:16
  173.4 4.7 %pad_maximum_fusion.2 = f32[320,4,1024]{2,0,1:T(8,128)} fusion(f32[320,1,1024]{2,0,1:T(8,128)} %get-tuple-element.7, f32[320,1,1024]{2,0,1:T(8,128)} %get-tuple-element.8, f32[320,1,1024]{2,0,1:T(8,128)S(1)} %get-tuple-element.6, f32[320,1,1024]{2,0,1:T(8,128)S(1)} %get-tuple-element.5), kind=kLoop, calls=%fused_computation.2 | loop fusion | flops 3932160 | bytes 10485760 | tf_op jit(solution)/shard_map/stack | solution.py:25
  178.1 8.2 %copy.51 = f32[320,4,1024]{2,1,0:T(4,128)} copy(f32[320,4,1024]{2,0,1:T(8,128)} %pad_maximum_fusion.2) | data formatting | bytes 10485760 | tf_op jit(solution)/shard_map/stack | solution.py:25
  186.3 7.3 %reshape_reshape.11 = f32[1280,1024]{1,0:T(8,128)} reshape(f32[320,4,1024]{2,1,0:T(4,128)} %copy.51) | data formatting | bytes 10485760 | tf_op jit(solution)/shard_map/reshape;reshape | solution.py:31
  193.7 3.3 fusion
  197.0 0.0 collective-permute-done
  197.1 0.1 add_select_fusion.3
  197.1 3.2 collective-permute-start.1
  200.3 2.7 collective-permute-done.1
  203.1 4.2 %collective-permute-start.2 = (f32[16,1280]{1,0:T(8,128)S(1)}, f32[16,1280]{1,0:T(8,128)S(1)}, u32[]{:S(2)}, u32[]{:S(2)}) collective-permute-start(f32[16,1280]{1,0:T(8,128)S(1)} %add_select_fusion.2), channel_id=1, source_target_pairs={{0,4},{4,0},{1,5},{5,1},{2,6},{6,2},{3,7},{7,3},{8,12},{12,8},{9,1... | collective-permute-start | bytes 245768 | tf_op jit(solution)/shard_map/ppermute | solution.py:16
  207.3 1.9 collective-permute-done.2
  209.2 7.4 %collective-permute-start.3 = (f32[16,1280]{1,0:T(8,128)S(1)}, f32[16,1280]{1,0:T(8,128)S(1)}, u32[]{:S(2)}, u32[]{:S(2)}) collective-permute-start(f32[16,1280]{1,0:T(8,128)S(1)} %add_select_fusion.1), channel_id=1, source_target_pairs={{0,8},{8,0},{1,9},{9,1},{2,10},{10,2},{3,11},{11,3},{4,12},{12,4},... | collective-permute-start | bytes 245768 | tf_op jit(solution)/shard_map/ppermute | solution.py:16
  216.6 1.8 collective-permute-done.3
  218.4 19.0 %collective-permute-start.4 = (f32[16,1280]{1,0:T(8,128)S(1)}, f32[16,1280]{1,0:T(8,128)S(1)}, u32[]{:S(2)}, u32[]{:S(2)}) collective-permute-start(f32[16,1280]{1,0:T(8,128)S(1)} %add_select_fusion), channel_id=1, source_target_pairs={{0,16},{16,0},{1,17},{17,1},{2,18},{18,2},{3,19},{19,3},{4,20},{20... | collective-permute-start | bytes 245768 | tf_op jit(solution)/shard_map/ppermute | solution.py:16
  237.4 2.3 collective-permute-done.4
  239.7 0.4 fusion.4
  240.1 18.4 %all_gather.7 = bf16[256,1280]{1,0:T(8,128)(2,1)S(1)} all-gather(bf16[16,1280]{1,0:T(8,128)(2,1)S(1)} %bitcast.76), channel_id=1, replica_groups=mesh['hid'=16,'inter'=32] {'hid'}, dimensions={0}, use_global_device_ids=true | all-gather | bytes 696320 | tf_op jit(solution)/shard_map/all_gather | solution.py:88
  258.5 1.9 fusion.51
  260.4 0.0 reduce-scatter.5.cloned.1.call-update
  260.4 109.5 %reduce-scatter.5.cloned.1.call-done = f32[8,1024]{1,0:T(8,128)} async-done(((f32[256,1024]{1,0:T(8,128)}), f32[8,1024]{1,0:T(8,128)}) %reduce-scatter.5.cloned.1.call-update) | async-done | bytes 32784 | tf_op jit(solution)/shard_map/reduce_scatter | solution.py:90
  369.9 1.4 convert_element_type.61
  (34 shorter events, 0.1 us)
Async XLA Ops:
  6.5 161.4 %reduce-scatter.7.cloned.1.call-start = ((), (), s32[]{:S(2)}) async-start(), calls=%async_computation.3 | async-start | bytes 2785280 | tf_op jit(solution)/shard_map/reduce_scatter | solution.py:75
  14.8 7.4 %copy-start.3 = (s32[8,1280]{1,0:T(8,128)S(1)}, s32[8,1280]{1,0:T(8,128)}, u32[]{:S(2)}) copy-start(s32[8,1280]{1,0:T(8,128)} %param.14) | copy-start | bytes 122884
  14.8 7.4 %copy-start.6 = (bf16[8,1280]{1,0:T(8,128)(2,1)S(1)}, bf16[8,1280]{1,0:T(8,128)(2,1)}, u32[]{:S(2)}) copy-start(bf16[8,1280]{1,0:T(8,128)(2,1)} %param.13) | copy-start | bytes 61444
  14.8 7.4 %copy-start.8 = (bf16[8,1024]{1,0:T(8,128)(2,1)S(1)}, bf16[8,1024]{1,0:T(8,128)(2,1)}, u32[]{:S(2)}) copy-start(bf16[8,1024]{1,0:T(8,128)(2,1)} %param.11) | copy-start | bytes 49156
  14.8 46.6 %copy-start = (f32[256,1280]{1,0:T(8,128)S(1)}, f32[256,1280]{1,0:T(8,128)}, u32[]{:S(2)}) copy-start(f32[256,1280]{1,0:T(8,128)} %param.15) | copy-start | bytes 3932164
  68.3 7.3 %copy-start.4 = (s32[8,1280]{1,0:T(8,128)S(1)}, s32[8,1280]{1,0:T(8,128)}, u32[]{:S(2)}) copy-start(s32[8,1280]{1,0:T(8,128)} %param.17) | copy-start | bytes 122884
  68.3 7.3 %copy-start.7 = (bf16[8,1280]{1,0:T(8,128)(2,1)S(1)}, bf16[8,1280]{1,0:T(8,128)(2,1)}, u32[]{:S(2)}) copy-start(bf16[8,1280]{1,0:T(8,128)(2,1)} %param.16) | copy-start | bytes 61444
  75.5 4.1 %slice-start = ((s8[5242880]{0:T(1024)(128)(4,1)}), s8[4194304]{0:T(1024)(128)(4,1)S(1)}, s32[]{:S(2)}) async-start(s8[5242880]{0:T(1024)(128)(4,1)} %bitcast.74), calls=%async_computation.4 | async-start | bytes 8388608
  75.6 4.1 %slice-start.1 = ((s8[5242880]{0:T(1024)(128)(4,1)}), s8[1048576]{0:T(1024)(128)(4,1)S(1)}, s32[]{:S(2)}) async-start(s8[5242880]{0:T(1024)(128)(4,1)} %bitcast.74), calls=%async_computation.5 | async-start | bytes 2097152
  83.4 0.7 copy-start.9
  83.4 286.5 %reduce-scatter.5.cloned.1.call-start = ((), (), s32[]{:S(2)}) async-start(), calls=%async_computation.2 | async-start | bytes 1081344 | tf_op jit(solution)/shard_map/reduce_scatter | solution.py:90
  168.9 28.1 %collective-permute-start = (f32[16,1280]{1,0:T(8,128)S(1)}, f32[16,1280]{1,0:T(8,128)S(1)}, u32[]{:S(2)}, u32[]{:S(2)}) collective-permute-start(f32[16,1280]{1,0:T(8,128)S(1)} %fusion.7), channel_id=1, source_target_pairs={{0,1},{1,0},{2,3},{3,2},{4,5},{5,4},{6,7},{7,6},{8,9},{9,8},{10,11... | collective-permute-start | bytes 245768 | tf_op jit(solution)/shard_map/ppermute | solution.py:16
  186.3 7.3 %copy-start.2 = (s32[10,1024]{1,0:T(8,128)S(1)}, s32[10,1024]{1,0:T(8,128)}, u32[]{:S(2)}) copy-start(s32[10,1024]{1,0:T(8,128)} %param.21) | copy-start | bytes 122884
  186.3 7.3 %copy-start.5 = (bf16[10,1024]{1,0:T(8,128)(2,1)S(1)}, bf16[10,1024]{1,0:T(8,128)(2,1)}, u32[]{:S(2)}) copy-start(bf16[10,1024]{1,0:T(8,128)(2,1)} %param.20) | copy-start | bytes 61444
  193.7 3.4 copy-start.1
  197.1 6.0 %collective-permute-start.1 = (f32[16,1280]{1,0:T(8,128)S(1)}, f32[16,1280]{1,0:T(8,128)S(1)}, u32[]{:S(2)}, u32[]{:S(2)}) collective-permute-start(f32[16,1280]{1,0:T(8,128)S(1)} %add_select_fusion.3), channel_id=1, source_target_pairs={{0,2},{2,0},{1,3},{3,1},{4,6},{6,4},{5,7},{7,5},{8,10},{10,8},{9,1... | collective-permute-start | bytes 245768 | tf_op jit(solution)/shard_map/ppermute | solution.py:16
  203.1 6.1 %collective-permute-start.2 = (f32[16,1280]{1,0:T(8,128)S(1)}, f32[16,1280]{1,0:T(8,128)S(1)}, u32[]{:S(2)}, u32[]{:S(2)}) collective-permute-start(f32[16,1280]{1,0:T(8,128)S(1)} %add_select_fusion.2), channel_id=1, source_target_pairs={{0,4},{4,0},{1,5},{5,1},{2,6},{6,2},{3,7},{7,3},{8,12},{12,8},{9,1... | collective-permute-start | bytes 245768 | tf_op jit(solution)/shard_map/ppermute | solution.py:16
  209.2 9.2 %collective-permute-start.3 = (f32[16,1280]{1,0:T(8,128)S(1)}, f32[16,1280]{1,0:T(8,128)S(1)}, u32[]{:S(2)}, u32[]{:S(2)}) collective-permute-start(f32[16,1280]{1,0:T(8,128)S(1)} %add_select_fusion.1), channel_id=1, source_target_pairs={{0,8},{8,0},{1,9},{9,1},{2,10},{10,2},{3,11},{11,3},{4,12},{12,4},... | collective-permute-start | bytes 245768 | tf_op jit(solution)/shard_map/ppermute | solution.py:16
  218.4 21.3 %collective-permute-start.4 = (f32[16,1280]{1,0:T(8,128)S(1)}, f32[16,1280]{1,0:T(8,128)S(1)}, u32[]{:S(2)}, u32[]{:S(2)}) collective-permute-start(f32[16,1280]{1,0:T(8,128)S(1)} %add_select_fusion), channel_id=1, source_target_pairs={{0,16},{16,0},{1,17},{17,1},{2,18},{18,2},{3,19},{19,3},{4,20},{20... | collective-permute-start | bytes 245768 | tf_op jit(solution)/shard_map/ppermute | solution.py:16
Sparse Core Ops, SparseCore 0:
  83.5 84.3 reduce-scatter.6
  260.5 109.3 reduce-scatter.4
where the time goes:
time: 381 us; the launch traced here: 378 us
  waiting for transfers between devices  198 us (52%)
  blocking collectives  57.6 us (15%)
  local copies, waits for them, and re-layouts  44.4 us (12%)
  starting transfers between devices  38.3 us (10%)
  other arithmetic  21.7 us (6%)
  between operations  13.7 us (4%)
  matrix products  4.05 us (1%)
    reduce_scatter x1, waiting for transfers between devices, body(): lax.psum_scatter(jnp.dot(full_rows, down_weight, preferred_element_type=j...  110 us
    reduce_scatter x1, waiting for transfers between devices, body(): lax.psum_scatter(partial_sums, 'hid', scatter_dimension=0, tiled=True)  80.1 us
    all_gather x1, blocking collectives, body(): piece = lax.all_gather(tokens, 'inter', axis=0, tiled=True)  39.2 us
    ppermute x5, starting transfers between devices, swapped(): return lax.ppermute(block, axis, route)  38.2 us
    another operation x3, local copies, waits for them, and re-layouts, dequantize(): grouped = code_values.reshape(groups, 128, code_values.shape[1])  22 us
    another operation x3, local copies, waits for them, and re-layouts, unpack_codes(): jnp.stack(pieces, axis=1).reshape(packed.shape[0] * 4, packed.shape[1])  19.7 us
    all_gather x1, blocking collectives, body(): full_rows = lax.all_gather(rotated, 'hid', axis=0, tiled=True)  18.4 us
    another operation x6, other arithmetic, unpack_codes(): jnp.stack(pieces, axis=1).reshape(packed.shape[0] * 4, packed.shape[1])  12 us
  transfers between devices with their start and end apart: 7, of which 6 were waited for; matrix products, arithmetic and copies ran while one was open for 7% of the time, Pallas kernels for 0%

commit v1 on v0

v1 whole, which is shorter than its diff:
```python
import functools

import jax
import jax.numpy as jnp
from jax import lax
from jax.experimental import pallas as pl
from jax.experimental.pallas import tpu as pltpu
from jax.sharding import PartitionSpec as P

MESH = pl.DeviceIdType.MESH
F32 = jnp.float32
BF16 = jnp.bfloat16
NH, NZ, NJ, NB = 16, 16, 32, 10


def slot_of(d):
    return (d + 3) % 16


def wait_bytes(view, sem):
    pltpu.make_async_copy(view, view, sem).wait()


def loop(lo, hi, fn):
    def step(i, carry):
        fn(i)
        return carry

    lax.fori_loop(lo, hi, step, 0)


def dequantized(words, zero, scale):
    w = words.astype(jnp.int32)
    planes = []
    for k in range(4):
        d = jnp.right_shift(w, 4 * k) if k else w
        if k < 3:
            d = jnp.bitwise_and(d, 15)
        planes.append(((d.astype(F32) - zero) * scale).astype(BF16))
    return planes


def kernel(
    tok, gw_hbm, gs, gz, uw_hbm, us, uz, sb, dw_hbm, ds, dz,
    out,
    gw, uw, dw, gsf, gzf, usf, uzf, dsf, dzf, sgn,
    W, Wd, X, L, S, B, U, C1, C2, R2, R, Lown, Loth, EXs, EXr, Pown, SB2, SB8, G, G8, T4, Fr,
    w_sem, as1, as2, asc, ar, arc, bs, br, c1s, c1r, c2s, c2r, dsd, drv, e1s, e1r, e2s, e2r, e3s, e3r,
):
    h = lax.axis_index("hid")
    j = lax.axis_index("inter")
    z = lax.div(j, 2)
    c = lax.rem(j, 2)
    oc = 1 - c

    def zdev(d):
        return (h, 2 * lax.rem(z + d + 16, 16) + c)

    other = (h, 2 * z + oc)

    def rcopy(src, dst, ss, rs, dev):
        return pltpu.make_async_remote_copy(
            src_ref=src, dst_ref=dst, send_sem=ss, recv_sem=rs, device_id=dev, device_id_type=MESH
        )

    loads = [
        pltpu.make_async_copy(gw_hbm, gw, w_sem.at[0]),
        pltpu.make_async_copy(uw_hbm, uw, w_sem.at[1]),
        pltpu.make_async_copy(dw_hbm, dw, w_sem.at[2]),
    ]
    for cp in loads:
        cp.start()

    bar = pltpu.get_barrier_semaphore()
    loop(1, NJ, lambda i: pl.semaphore_signal(
        bar, inc=1, device_id=(h, lax.rem(j + i, NJ)), device_id_type=MESH))
    loop(1, NH, lambda i: pl.semaphore_signal(
        bar, inc=1, device_id=(lax.rem(h + i, NH), j), device_id_type=MESH))

    rows = lax.broadcasted_iota(jnp.int32, (128, 128), 0)
    cols = lax.broadcasted_iota(jnp.int32, (128, 128), 1)
    place = 32 * jnp.bitwise_and(rows, 3) + jnp.right_shift(rows, 2)
    shuffle = jnp.where(place == cols, 1.0, 0.0).astype(BF16)
    for g in range(4):
        both = [
            jnp.dot(tok[:, 512 * u + 128 * g:512 * u + 128 * g + 128], shuffle, preferred_element_type=F32)
            for u in range(2)
        ]
        X[3, c, g] = jnp.concatenate(both, axis=0).astype(BF16)

    gsf[...] = gs[...].astype(F32)
    usf[...] = us[...].astype(F32)
    gzf[...] = gz[...].astype(F32)
    uzf[...] = uz[...].astype(F32)
    dsv, dzv, sgv = ds[...].astype(F32), dz[...].astype(F32), (1 - 2 * sb[...]).astype(F32)
    for b in range(NB):
        dsf[b], dzf[b], sgn[b] = dsv[b:b + 1], dzv[b:b + 1], sgv[b:b + 1]

    pl.semaphore_wait(bar, NJ - 1 + NH - 1)

    first = (4, -4, 1, -1, 2, -2, 3, -3)
    stage1 = [
        rcopy(X.at[3, c], X.at[slot_of(-e), c], as1.at[k], ar.at[slot_of(-e)], zdev(e))
        for k, e in enumerate(first)
    ]
    for cp in stage1:
        cp.start()

    def to_core(s):
        return rcopy(X.at[s, c], X.at[s, c], asc, arc.at[s // 8], other)

    to_core(3).start()

    def arrived(s):
        wait_bytes(X.at[s, c], ar.at[s])

    def dequant_gu(b):
        at = pl.ds(pl.multiple_of(b * 128, 128), 128)
        for words, zf, sf, lane in ((gw, gzf, gsf, 0), (uw, uzf, usf, 128)):
            for g in range(8):
                planes = dequantized(words[32 * g:32 * g + 32, at], zf[g:g + 1, at], sf[g:g + 1, at])
                for k in range(4):
                    W[b, 128 * g + 32 * k:128 * g + 32 * k + 32, lane:lane + 128] = planes[k]

    loads[0].wait()
    loads[1].wait()
    loop(0, 4, dequant_gu)

    stage2 = []
    for way in (1, -1):
        s = slot_of(-4 * way)
        arrived(s)
        for e in (1, 2, 3):
            to = slot_of(-(4 + e) * way)
            stage2.append(rcopy(X.at[s, c], X.at[to, c], as2.at[len(stage2)], ar.at[to], zdev(e * way)))
        half = 0 if way == 1 else 1
        stage2.append(rcopy(
            X.at[s, c, pl.ds(2 * half, 2)], X.at[slot_of(8), c, pl.ds(2 * half, 2)],
            as2.at[len(stage2)], ar.at[16 + half], zdev(4 * way)))
        for cp in stage2[-4:]:
            cp.start()
    to_core(slot_of(4)).start()
    to_core(slot_of(-4)).start()
    for e in (1, -1, 2, -2, 3, -3):
        arrived(slot_of(e))
        to_core(slot_of(e)).start()

    loop(4, NB, dequant_gu)

    for e in (5, -5, 6, -6, 7, -7):
        arrived(slot_of(e))
        to_core(slot_of(e)).start()
    for half in range(2):
        wait_bytes(X.at[slot_of(8), c, pl.ds(2 * half, 2)], ar.at[16 + half])
    to_core(slot_of(8)).start()

    for part in range(2):
        wait_bytes(X.at[pl.ds(8 * part, 8), oc], arc.at[part])

        def lay(s, part=part):
            at = pl.ds(pl.multiple_of(16 * s, 16), 16)
            for g in range(4):
                t0 = X[8 * part + s, 0, g].astype(F32)
                t1 = X[8 * part + s, 1, g].astype(F32)
                L[at, 128 * g:128 * g + 128] = jnp.concatenate([t0[:8], t1[:8]], axis=0).astype(BF16)
                L[at, 512 + 128 * g:640 + 128 * g] = jnp.concatenate([t0[8:], t1[8:]], axis=0).astype(BF16)

        loop(0, 8, lay)

        def product(b, part=part):
            v = jnp.dot(L[...], W[b], preferred_element_type=F32).astype(BF16)
            for s in range(8):
                r = 10 * s + b
                for u in range(2):
                    S[part, lax.div(r, 16), lax.rem(r, 16), u] = v[16 * s:16 * s + 16, 128 * u:128 * u + 128]

        loop(0, NB, product)

        n0 = 10 * lax.rem(z + 13 + 8 * part, 16)

        def send(p, part=part, n0=n0):
            y = lax.rem(lax.div(h, 4) + lax.div(p, 4), 4)
            x = lax.rem(lax.rem(h, 4) + lax.rem(p, 4), 4)
            to = 4 * y + x
            r0 = lax.rem(to - n0 + 160, 16)
            rcopy(S.at[part, :, r0], B.at[part, h], bs.at[part], br.at[part], (to, j)).start()

        loop(1, NH, send)
        B[part, h] = S[part, :, lax.rem(h - n0 + 160, 16)]

    loads[2].wait()

    def dequant_d(b):
        at = pl.ds(pl.multiple_of(b * 32, 32), 32)
        for q in range(8):
            lanes = slice(128 * q, 128 * q + 128)
            planes = dequantized(dw[at, lanes], dzf[b, :, lanes], dsf[b, :, lanes])
            for k in range(4):
                to = pl.ds(pl.multiple_of(b * 128 + 32 * k, 32), 32)
                Wd[q // 2, to, 128 * (q % 2):128 * (q % 2) + 128] = planes[k]

    loop(0, NB, dequant_d)

    for cp in stage1 + stage2:
        cp.wait_send()
    wait_bytes(X.at[:, c], asc)

    for part in range(2):
        wait_bytes(B.at[part, pl.ds(0, NH - 1)], br.at[part])
        n0 = 10 * lax.rem(z + 13 + 8 * part, 16)
        r0 = lax.rem(h - n0 + 160, 16)

        def unit(q, part=part, n0=n0, r0=r0):
            n = lax.rem(n0 + r0 + 16 * q, 160)
            total = B[part, 0, q].astype(F32)
            for s in range(1, NH):
                total = total + B[part, s, q].astype(F32)
            gate, up = total[0], total[1]
            hidden = gate / (1.0 + jnp.exp(-gate)) * up
            U[lax.div(n, 16)] = (hidden * sgn[lax.rem(n, 10)]).astype(BF16)

        loop(0, 5, unit)

    def collect(m):
        owner = 3 * m + 1

        @pl.when(owner != j)
        def _():
            rcopy(U.at[m], C1.at[j], c1s.at[m], c1r, (h, owner)).start()

        @pl.when(owner == j)
        def _():
            C1[j] = U[m]

    loop(0, NB, collect)

    owns = jnp.logical_and(lax.rem(j, 3) == 1, j <= 28)
    mine = lax.div(j, 3)

    @pl.when(owns)
    def _():
        turned = 4 * jnp.bitwise_and(cols, 31) + jnp.right_shift(cols, 5)
        common = jnp.bitwise_and(rows, turned)
        odd = jnp.zeros_like(common)
        for bit in range(7):
            odd = jnp.bitwise_xor(odd, jnp.right_shift(common, bit))
        factor = (1 - 2 * jnp.bitwise_and(odd, 1)).astype(F32).astype(BF16)
        wait_bytes(C1.at[pl.ds(0, NJ - 1)], c1r)
        vals = [jnp.dot(C1[i], factor, preferred_element_type=F32) for i in range(NJ)]
        step = 1
        while step < NJ:
            vals = [
                vals[i] + vals[i ^ step] if not i & step else vals[i ^ step] - vals[i] for i in range(NJ)
            ]
            step *= 2
        for i in range(NJ):
            C2[i] = (vals[i] * (1.0 / 64.0)).astype(BF16)

        def back(p):
            i = lax.rem(j + p, NJ)
            rcopy(C2.at[i], R2.at[mine], c2s, c2r, (h, i)).start()

        loop(1, NJ, back)
        R2[mine] = C2[j]
        wait_bytes(R2.at[pl.ds(0, NB - 1)], c2r)

    @pl.when(jnp.logical_not(owns))
    def _():
        wait_bytes(R2.at[pl.ds(0, NB)], c2r)

    def spread(p):
        y = lax.rem(lax.div(h, 4) + lax.div(p, 4), 4)
        x = lax.rem(lax.rem(h, 4) + lax.rem(p, 4), 4)
        rcopy(R2, R.at[:, h], dsd, drv, (4 * y + x, j)).start()

    loop(1, NH, spread)
    for m in range(NB):
        R[m, h] = R2[m]

    for part in range(2):
        wait_bytes(S.at[part, :, pl.ds(0, NH - 1)], bs.at[part])

    def collected(m):
        @pl.when(3 * m + 1 != j)
        def _():
            wait_bytes(U.at[m], c1s.at[m])

    loop(0, NB, collected)

    @pl.when(owns)
    def _():
        wait_bytes(C2.at[pl.ds(0, NJ - 1)], c2s)

    wait_bytes(R.at[:, pl.ds(0, NH - 1)], drv)

    def split(a):
        at = pl.ds(pl.multiple_of(16 * a, 16), 16)
        for b in range(NB):
            n = 20 * a + b
            t0 = R[lax.div(n, 16), lax.rem(n, 16)].astype(F32)
            t1 = R[lax.div(n + 10, 16), lax.rem(n + 10, 16)].astype(F32)
            low = jnp.concatenate([t0[:8], t1[:8]], axis=0)
            high = jnp.concatenate([t0[8:], t1[8:]], axis=0)
            lanes = slice(128 * b, 128 * b + 128)
            Lown[at, lanes] = jnp.where(c == 0, low, high).astype(BF16)
            Loth[at, lanes] = jnp.where(c == 0, high, low).astype(BF16)

    loop(0, 8, split)

    def pair(lhs, i):
        lo = jnp.dot(lhs[...], Wd[i], preferred_element_type=F32).reshape(NZ, 8, 256)
        hi = jnp.dot(lhs[...], Wd[2 + i], preferred_element_type=F32).reshape(NZ, 8, 256)
        return jnp.concatenate([lo, hi], axis=1)

    def for_other(i):
        EXs[i] = pair(Loth, i).astype(BF16)
        rcopy(EXs.at[i], EXr.at[i], e1s.at[i], e1r.at[i], other).start()

    loop(0, 2, for_other)

    def for_own(i):
        Pown[i] = pair(Lown, i)

    loop(0, 2, for_own)

    for i in range(2):
        wait_bytes(EXr.at[i], e1r.at[i])

    def block(d, i):
        at = lax.rem(z + d + 16, 16)
        return Pown[i, at] + EXr[i, at].astype(F32)

    SB8[0] = block(8, 0).astype(BF16)
    SB8[1] = block(8, 1).astype(BF16)
    sends = [
        rcopy(SB8.at[0], G8.at[0], e2s.at[6], e2r.at[6], zdev(4)),
        rcopy(SB8.at[1], G8.at[1], e2s.at[7], e2r.at[7], zdev(-4)),
    ]
    sends[0].start()
    sends[1].start()
    for e in (3, 2, 1):
        for way in (1, -1):
            k = e - 1 if way == 1 else 2 + e
            for i in range(2):
                SB2[k, 0, i] = block(e * way, i).astype(BF16)
                SB2[k, 1, i] = block((e + 4) * way, i).astype(BF16)
            cp = rcopy(SB2.at[k], G.at[k], e2s.at[k], e2r.at[k], zdev(e * way))
            cp.start()
            sends.append(cp)

    for k in range(6):
        wait_bytes(G.at[k], e2r.at[k])
    for k in range(2):
        wait_bytes(G8.at[k], e2r.at[6 + k])
    for side, way in ((0, 1), (1, -1)):
        for i in range(2):
            total = block(4 * way, i)
            for k in range(3):
                total = total + G[3 * side + k, 1, i].astype(F32)
            if i == side:
                total = total + G8[side].astype(F32)
            T4[side, i] = total.astype(BF16)
        cp = rcopy(T4.at[side], Fr.at[side], e3s.at[side], e3r.at[side], zdev(4 * way))
        cp.start()
        sends.append(cp)

    totals = []
    for i in range(2):
        total = block(0, i)
        for k in range(6):
            total = total + G[k, 0, i].astype(F32)
        totals.append(total)
    for cp in sends:
        cp.wait_send()
    for i in range(2):
        wait_bytes(EXs.at[i], e1s.at[i])
    wait_bytes(R.at[:, pl.ds(0, NH - 1)], dsd)
    for side in range(2):
        wait_bytes(Fr.at[side], e3r.at[side])
    for i in range(2):
        total = totals[i] + Fr[0, i].astype(F32) + Fr[1, i].astype(F32)
        out[:, 256 * i:256 * i + 256] = total[:8].astype(BF16)
        out[:, 512 + 256 * i:768 + 256 * i] = total[8:].astype(BF16)


def body(tok, gw, gs, gz, uw, us, uz, sb, dw, ds, dz):
    vmem = pl.BlockSpec(memory_space=pltpu.VMEM)
    hbm = pl.BlockSpec(memory_space=pl.ANY)
    V = pltpu.VMEM
    D = pltpu.SemaphoreType.DMA
    return pl.pallas_call(
        kernel,
        out_shape=jax.ShapeDtypeStruct((8, 1024), BF16),
        in_specs=[vmem, hbm, vmem, vmem, hbm, vmem, vmem, vmem, hbm, vmem, vmem],
        out_specs=vmem,
        scratch_shapes=[
            V((256, 1280), F32), V((256, 1280), F32), V((320, 1024), F32),
            V((8, 1280), F32), V((8, 1280), F32), V((8, 1280), F32), V((8, 1280), F32),
            V((10, 1, 1024), F32), V((10, 1, 1024), F32), V((10, 1, 128), F32),
            V((10, 1024, 256), BF16),
            V((4, 1280, 256), BF16),
            V((16, 2, 4, 16, 128), BF16),
            V((128, 1024), BF16),
            V((2, 5, 16, 2, 16, 128), BF16),
            V((2, 16, 5, 2, 16, 128), BF16),
            V((10, 16, 128), BF16),
            V((32, 16, 128), BF16),
            V((32, 16, 128), BF16),
            V((10, 16, 128), BF16),
            V((10, 16, 16, 128), BF16),
            V((128, 1280), BF16), V((128, 1280), BF16),
            V((2, 16, 16, 256), BF16), V((2, 16, 16, 256), BF16),
            V((2, 16, 16, 256), F32),
            V((6, 2, 2, 16, 256), BF16), V((2, 16, 256), BF16),
            V((6, 2, 2, 16, 256), BF16), V((2, 16, 256), BF16),
            V((2, 2, 16, 256), BF16), V((2, 2, 16, 256), BF16),
            D((3,)), D((8,)), D((8,)), D, D((18,)), D((2,)), D((2,)), D((2,)),
            D((10,)), D, D, D, D, D, D((2,)), D((2,)), D((8,)), D((8,)), D((2,)), D((2,)),
        ],
        compiler_params=pltpu.CompilerParams(
            collective_id=0, has_side_effects=True, vmem_limit_bytes=48 * 1024 * 1024
        ),
        name="rotated_ffn",
    )(tok, gw, gs, gz, uw, us, uz, sb.reshape(10, 128), dw, ds, dz)


def solution(mesh):
    in_specs = (
        P("inter", "hid"),
        P("hid", "inter"),
        P("hid", "inter"),
        P("hid", "inter"),
        P("hid", "inter"),
        P("hid", "inter"),
        P("hid", "inter"),
        P("inter"),
        P("inter", "hid"),
        P("inter", "hid"),
        P("inter", "hid"),
    )
    return jax.shard_map(
        body, mesh=mesh, in_specs=in_specs, out_specs=P("inter", "hid"), check_vma=False
    )
```

time: 381 us -> 99.6 us (0.26)
  waiting for transfers between devices: 198 us -> 0 us
  Pallas kernels: 0 us -> 88.3 us
  blocking collectives: 57.6 us -> 0 us
  starting transfers between devices: 38.3 us -> 0 us
  local copies, waits for them, and re-layouts: 44.4 us -> 10.6 us
  other arithmetic: 21.7 us -> 0 us
  between operations: 13.7 us -> 0.02 us
  matrix products: 4.05 us -> 0 us
    reduce_scatter x2 -> x0, waiting for transfers between devices: 190 us -> none  [the longest x1 110 us: body(): lax.psum_scatter(jnp.dot(full_rows, down_weight, preferred_element_type=j...]
    pallas_call x0 -> x1, Pallas kernels: none -> 88.3 us  [body(): pl.pallas_call(kernel, out_shape=jax.ShapeDtypeStruct((8, 1024), BF16), i...]
    all_gather x2 -> x0, blocking collectives: 57.6 us -> none  [the longest x1 39.2 us: body(): piece = lax.all_gather(tokens, 'inter', axis=0, tiled=True)]
    another operation x6 -> x0, local copies, waits for them, and re-layouts: 41.7 us -> none  [the longest x3 22 us: dequantize(): grouped = code_values.reshape(groups, 128, code_values.shape[1])]
    ppermute x5 -> x0, starting transfers between devices: 38.2 us -> none  [swapped(): return lax.ppermute(block, axis, route)]
    another operation x6 -> x0, other arithmetic: 12 us -> none  [unpack_codes(): jnp.stack(pieces, axis=1).reshape(packed.shape[0] * 4, packed.shape[1])]
    ppermute x5 -> x0, waiting for transfers between devices: 8.71 us -> none  [swapped(): return lax.ppermute(block, axis, route)]
    convert_element_type x11 -> x0, other arithmetic: 8.45 us -> none  [the longest x3 7.04 us: dequantize(): weight.reshape(groups * 128, code_values.shape[1]).astype(jnp.bfloat16)]
  transfers between devices with their start and end apart: 7 -> 0, of which waited for: 6 -> 0; matrix products, arithmetic and copies ran while one was open for 7% -> 0% of each run, Pallas kernels for 0% -> 0%
where the time goes in v1:
time: 99.6 us; the launch traced here: 98.9 us
  Pallas kernels  88.3 us (89%)
  local copies, waits for them, and re-layouts  10.6 us (11%)
    pallas_call x1, Pallas kernels, body(): pl.pallas_call(kernel, out_shape=jax.ShapeDtypeStruct((8, 1024), BF16), i...  88.3 us
    unnamed x23, local copies, waits for them, and re-layouts  10.6 us

profile of v1, /device:TPU:1, one launch (start us, length us, event | category | flops | bytes accessed | tf_op | source)
XLA Modules:
  0.0 98.9 jit_solution(1426698567810803252)
XLA Ops:
  0.0 0.0 copy-start
  0.0 1.3 %copy-done = f32[256,1280]{1,0:T(8,128)S(1)} copy-done((f32[256,1280]{1,0:T(8,128)S(1)}, f32[256,1280]{1,0:T(8,128)}, u32[]{:S(2)}) %copy-start) | copy-done | bytes 1310744
  1.3 0.0 copy-start.1
  1.3 1.3 %copy-done.1 = f32[256,1280]{1,0:T(8,128)S(1)} copy-done((f32[256,1280]{1,0:T(8,128)S(1)}, f32[256,1280]{1,0:T(8,128)}, u32[]{:S(2)}) %copy-start.1) | copy-done | bytes 1310744
  2.6 0.0 copy-start.2
  2.6 1.3 %copy-done.2 = f32[320,1024]{1,0:T(8,128)S(1)} copy-done((f32[320,1024]{1,0:T(8,128)S(1)}, f32[320,1024]{1,0:T(8,128)}, u32[]{:S(2)}) %copy-start.2) | copy-done | bytes 1310744
  4.0 0.0 copy-start.3
  4.0 0.8 copy-done.3
  4.8 0.0 copy-start.4
  4.8 0.8 copy-done.4
  5.6 0.0 copy-start.5
  5.6 0.8 copy-done.5
  6.3 0.0 copy-start.6
  6.4 0.8 copy-done.6
  7.1 0.0 copy-start.7
  7.1 0.7 copy-done.7
  7.8 0.0 copy-start.8
  7.8 0.7 copy-done.8
  8.6 0.0 copy-start.9
  8.6 0.7 copy-done.9
  9.3 0.0 copy-start.10
  9.3 0.7 copy-done.10
  10.0 88.3 %rotated_ffn.1 = bf16[8,1024]{1,0:T(8,128)(2,1)S(1)} custom-call(bf16[8,1024]{1,0:T(8,128)(2,1)S(1)} %copy-done.9, f32[256,1280]{1,0:T(8,128)S(1)} %copy-done, bf16[8,1280]{1,0:T(8,128)(2,1)S(1)} %copy-done.7, s32[8,1280]{1,0:T(8,128)S(1)} %copy-done.4, f32[256,1280]{1,0:T(8,128)S(1)} %copy-done.1, bf16[8,1280]{1,0:T(8,128)(2,1)S(1)} %copy-done.8, ...), custom_call_target="tpu_custom_call" | custom-call | tf_op jit(solution)/shard_map/rotated_ffn/pallas_call | solution.py:391
  98.3 0.6 copy.13
Async XLA Ops:
  0.0 1.3 %copy-start = (f32[256,1280]{1,0:T(8,128)S(1)}, f32[256,1280]{1,0:T(8,128)}, u32[]{:S(2)}) copy-start(f32[256,1280]{1,0:T(8,128)} %gw_hbm.1) | copy-start | bytes 3932164
  1.3 1.3 %copy-start.1 = (f32[256,1280]{1,0:T(8,128)S(1)}, f32[256,1280]{1,0:T(8,128)}, u32[]{:S(2)}) copy-start(f32[256,1280]{1,0:T(8,128)} %uw_hbm.1) | copy-start | bytes 3932164
  2.6 1.3 %copy-start.2 = (f32[320,1024]{1,0:T(8,128)S(1)}, f32[320,1024]{1,0:T(8,128)}, u32[]{:S(2)}) copy-start(f32[320,1024]{1,0:T(8,128)} %dw_hbm.1) | copy-start | bytes 3932164
  4.0 0.8 copy-start.3
  4.8 0.8 copy-start.4
  5.6 0.8 copy-start.5
  6.3 0.8 copy-start.6
  7.1 0.7 copy-start.7
  7.8 0.7 copy-start.8
  8.6 0.7 copy-start.9
  9.3 0.7 copy-start.10

commit v2 on v1

--- a/solution.py
+++ b/solution.py
@@ -41,12 +41,16 @@
 
 
 def kernel(
-    tok, gw_hbm, gs, gz, uw_hbm, us, uz, sb, dw_hbm, ds, dz,
-    out,
-    gw, uw, dw, gsf, gzf, usf, uzf, dsf, dzf, sgn,
+    *refs,
+):
+    inputs, out, scratch = refs[:11], refs[11], refs[12:]
+    held = scratch[:11]
+    tok, gw, gs, gz, uw, us, uz, sb, dw, ds, dz = held
+    (
+    gsf, gzf, usf, uzf, dsf, dzf, sgn,
     W, Wd, X, L, S, B, U, C1, C2, R2, R, Lown, Loth, EXs, EXr, Pown, SB2, SB8, G, G8, T4, Fr,
-    w_sem, as1, as2, asc, ar, arc, bs, br, c1s, c1r, c2s, c2r, dsd, drv, e1s, e1r, e2s, e2r, e3s, e3r,
-):
+    w_sem, as1, as2, asc, ar, arc, bs, br, c1s, c1r, c2s, c2r, dsd, drv, e1s, e1r, e2s, e2r, e8s, e8r, e3s, e3r,
+    ) = scratch[11:]
     h = lax.axis_index("hid")
     j = lax.axis_index("inter")
     z = lax.div(j, 2)
@@ -63,24 +67,23 @@
             src_ref=src, dst_ref=dst, send_sem=ss, recv_sem=rs, device_id=dev, device_id_type=MESH
         )
 
-    loads = [
-        pltpu.make_async_copy(gw_hbm, gw, w_sem.at[0]),
-        pltpu.make_async_copy(uw_hbm, uw, w_sem.at[1]),
-        pltpu.make_async_copy(dw_hbm, dw, w_sem.at[2]),
-    ]
-    for cp in loads:
-        cp.start()
-
+    near = (4, -4, 1, -1, 2, -2, 3, -3)
     bar = pltpu.get_barrier_semaphore()
-    loop(1, NJ, lambda i: pl.semaphore_signal(
-        bar, inc=1, device_id=(h, lax.rem(j + i, NJ)), device_id_type=MESH))
+    for d in near:
+        pl.semaphore_signal(bar, inc=1, device_id=zdev(d), device_id_type=MESH)
+    pl.semaphore_signal(bar, inc=1, device_id=other, device_id_type=MESH)
     loop(1, NH, lambda i: pl.semaphore_signal(
         bar, inc=1, device_id=(lax.rem(h + i, NH), j), device_id_type=MESH))
+
+    loads = [pltpu.make_async_copy(inputs[i], held[i], w_sem.at[i]) for i in range(11)]
+    for i in (0, 1, 4, 2, 3, 5, 6, 8, 7, 9, 10):
+        loads[i].start()
 
     rows = lax.broadcasted_iota(jnp.int32, (128, 128), 0)
     cols = lax.broadcasted_iota(jnp.int32, (128, 128), 1)
     place = 32 * jnp.bitwise_and(rows, 3) + jnp.right_shift(rows, 2)
     shuffle = jnp.where(place == cols, 1.0, 0.0).astype(BF16)
+    loads[0].wait()
     for g in range(4):
         both = [
             jnp.dot(tok[:, 512 * u + 128 * g:512 * u + 128 * g + 128], shuffle, preferred_element_type=F32)
@@ -88,20 +91,11 @@
         ]
         X[3, c, g] = jnp.concatenate(both, axis=0).astype(BF16)
 
-    gsf[...] = gs[...].astype(F32)
-    usf[...] = us[...].astype(F32)
-    gzf[...] = gz[...].astype(F32)
-    uzf[...] = uz[...].astype(F32)
-    dsv, dzv, sgv = ds[...].astype(F32), dz[...].astype(F32), (1 - 2 * sb[...]).astype(F32)
-    for b in range(NB):
-        dsf[b], dzf[b], sgn[b] = dsv[b:b + 1], dzv[b:b + 1], sgv[b:b + 1]
-
-    pl.semaphore_wait(bar, NJ - 1 + NH - 1)
-
-    first = (4, -4, 1, -1, 2, -2, 3, -3)
+    pl.semaphore_wait(bar, len(near) + 1 + NH - 1)
+
     stage1 = [
         rcopy(X.at[3, c], X.at[slot_of(-e), c], as1.at[k], ar.at[slot_of(-e)], zdev(e))
-        for k, e in enumerate(first)
+        for k, e in enumerate(near)
     ]
     for cp in stage1:
         cp.start()
@@ -122,9 +116,30 @@
                 for k in range(4):
                     W[b, 128 * g + 32 * k:128 * g + 32 * k + 32, lane:lane + 128] = planes[k]
 
-    loads[0].wait()
-    loads[1].wait()
-    loop(0, 4, dequant_gu)
+    for i in (1, 2, 3, 4, 5, 6):
+        loads[i].wait()
+    gsf[...] = gs[...].astype(F32)
+    usf[...] = us[...].astype(F32)
+    gzf[...] = gz[...].astype(F32)
+    uzf[...] = uz[...].astype(F32)
+    loop(0, NB, dequant_gu)
+
+    for i in (7, 8, 9, 10):
+        loads[i].wait()
+    dsv, dzv, sgv = ds[...].astype(F32), dz[...].astype(F32), (1 - 2 * sb[...]).astype(F32)
+    for b in range(NB):
+        dsf[b], dzf[b], sgn[b] = dsv[b:b + 1], dzv[b:b + 1], sgv[b:b + 1]
+
+    def dequant_d(b):
+        at = pl.ds(pl.multiple_of(b * 32, 32), 32)
+        for q in range(8):
+            lanes = slice(128 * q, 128 * q + 128)
+            planes = dequantized(dw[at, lanes], dzf[b, :, lanes], dsf[b, :, lanes])
+            for k in range(4):
+                to = pl.ds(pl.multiple_of(b * 128 + 32 * k, 32), 32)
+                Wd[q // 2, to, 128 * (q % 2):128 * (q % 2) + 128] = planes[k]
+
+    loop(0, NB, dequant_d)
 
     stage2 = []
     for way in (1, -1):
@@ -140,21 +155,19 @@
         for cp in stage2[-4:]:
             cp.start()
     to_core(slot_of(4)).start()
-    to_core(slot_of(-4)).start()
     for e in (1, -1, 2, -2, 3, -3):
         arrived(slot_of(e))
         to_core(slot_of(e)).start()
-
-    loop(4, NB, dequant_gu)
-
-    for e in (5, -5, 6, -6, 7, -7):
-        arrived(slot_of(e))
-        to_core(slot_of(e)).start()
-    for half in range(2):
-        wait_bytes(X.at[slot_of(8), c, pl.ds(2 * half, 2)], ar.at[16 + half])
-    to_core(slot_of(8)).start()
+    to_core(slot_of(-4)).start()
 
     for part in range(2):
+        if part == 1:
+            for e in (5, -5, 6, -6, 7, -7):
+                arrived(slot_of(e))
+                to_core(slot_of(e)).start()
+            for half in range(2):
+                wait_bytes(X.at[slot_of(8), c, pl.ds(2 * half, 2)], ar.at[16 + half])
+            to_core(slot_of(8)).start()
         wait_bytes(X.at[pl.ds(8 * part, 8), oc], arc.at[part])
 
         def lay(s, part=part):
@@ -188,22 +201,24 @@
         loop(1, NH, send)
         B[part, h] = S[part, :, lax.rem(h - n0 + 160, 16)]
 
-    loads[2].wait()
-
-    def dequant_d(b):
-        at = pl.ds(pl.multiple_of(b * 32, 32), 32)
-        for q in range(8):
-            lanes = slice(128 * q, 128 * q + 128)
-            planes = dequantized(dw[at, lanes], dzf[b, :, lanes], dsf[b, :, lanes])
-            for k in range(4):
-                to = pl.ds(pl.multiple_of(b * 128 + 32 * k, 32), 32)
-                Wd[q // 2, to, 128 * (q % 2):128 * (q % 2) + 128] = planes[k]
-
-    loop(0, NB, dequant_d)
-
     for cp in stage1 + stage2:
         cp.wait_send()
     wait_bytes(X.at[:, c], asc)
+
+    def owner_of(m, side):
+        return 8 * lax.div(m, 5) + lax.rem(m, 5) + 16 * side
+
+    def collect(m):
+        for side in range(2):
+            owner = owner_of(m, side)
+
+            @pl.when(owner != j)
+            def _():
+                rcopy(U.at[m], C1.at[j], c1s.at[2 * m + side], c1r, (h, owner)).start()
+
+            @pl.when(owner == j)
+            def _():
+                C1[j] = U[m]
 
     for part in range(2):
         wait_bytes(B.at[part, pl.ds(0, NH - 1)], br.at[part])
@@ -217,25 +232,14 @@
                 total = total + B[part, s, q].astype(F32)
             gate, up = total[0], total[1]
             hidden = gate / (1.0 + jnp.exp(-gate)) * up
-            U[lax.div(n, 16)] = (hidden * sgn[lax.rem(n, 10)]).astype(BF16)
+            m = lax.div(n, 16)
+            U[m] = (hidden * sgn[lax.rem(n, 10)]).astype(BF16)
+            collect(m)
 
         loop(0, 5, unit)
 
-    def collect(m):
-        owner = 3 * m + 1
-
-        @pl.when(owner != j)
-        def _():
-            rcopy(U.at[m], C1.at[j], c1s.at[m], c1r, (h, owner)).start()
-
-        @pl.when(owner == j)
-        def _():
-            C1[j] = U[m]
-
-    loop(0, NB, collect)
-
-    owns = jnp.logical_and(lax.rem(j, 3) == 1, j <= 28)
-    mine = lax.div(j, 3)
+    owns = lax.rem(j, 8) < 5
+    mine = 5 * lax.div(lax.rem(j, 16), 8) + lax.rem(j, 8)
 
     @pl.when(owns)
     def _():
@@ -256,11 +260,14 @@
         for i in range(NJ):
             C2[i] = (vals[i] * (1.0 / 64.0)).astype(BF16)
 
-        def back(p):
-            i = lax.rem(j + p, NJ)
-            rcopy(C2.at[i], R2.at[mine], c2s, c2r, (h, i)).start()
-
-        loop(1, NJ, back)
+        def back(q):
+            i = 2 * lax.rem(z + lax.div(q, 2) + 12, 16) + lax.rem(q, 2)
+
+            @pl.when(i != j)
+            def _():
+                rcopy(C2.at[i], R2.at[mine], c2s, c2r, (h, i)).start()
+
+        loop(0, 16, back)
         R2[mine] = C2[j]
         wait_bytes(R2.at[pl.ds(0, NB - 1)], c2r)
 
@@ -281,15 +288,16 @@
         wait_bytes(S.at[part, :, pl.ds(0, NH - 1)], bs.at[part])
 
     def collected(m):
-        @pl.when(3 * m + 1 != j)
-        def _():
-            wait_bytes(U.at[m], c1s.at[m])
+        for side in range(2):
+            @pl.when(owner_of(m, side) != j)
+            def _():
+                wait_bytes(U.at[m], c1s.at[2 * m + side])
 
     loop(0, NB, collected)
 
     @pl.when(owns)
     def _():
-        wait_bytes(C2.at[pl.ds(0, NJ - 1)], c2s)
+        wait_bytes(C2.at[pl.ds(0, 15)], c2s)
 
     wait_bytes(R.at[:, pl.ds(0, NH - 1)], drv)
 
@@ -318,67 +326,57 @@
 
     loop(0, 2, for_other)
 
-    def for_own(i):
-        Pown[i] = pair(Lown, i)
-
-    loop(0, 2, for_own)
-
-    for i in range(2):
-        wait_bytes(EXr.at[i], e1r.at[i])
-
     def block(d, i):
         at = lax.rem(z + d + 16, 16)
         return Pown[i, at] + EXr[i, at].astype(F32)
 
-    SB8[0] = block(8, 0).astype(BF16)
-    SB8[1] = block(8, 1).astype(BF16)
-    sends = [
-        rcopy(SB8.at[0], G8.at[0], e2s.at[6], e2r.at[6], zdev(4)),
-        rcopy(SB8.at[1], G8.at[1], e2s.at[7], e2r.at[7], zdev(-4)),
-    ]
-    sends[0].start()
-    sends[1].start()
-    for e in (3, 2, 1):
-        for way in (1, -1):
-            k = e - 1 if way == 1 else 2 + e
-            for i in range(2):
-                SB2[k, 0, i] = block(e * way, i).astype(BF16)
-                SB2[k, 1, i] = block((e + 4) * way, i).astype(BF16)
-            cp = rcopy(SB2.at[k], G.at[k], e2s.at[k], e2r.at[k], zdev(e * way))
+    sends = []
+    for i in range(2):
+        Pown[i] = pair(Lown, i)
+        wait_bytes(EXr.at[i], e1r.at[i])
+        SB8[i] = block(8, i).astype(BF16)
+        cp = rcopy(SB8.at[i], G8.at[i], e8s.at[i], e8r.at[i], zdev(4 if i == 0 else -4))
+        cp.start()
+        sends.append(cp)
+        for e in (3, 2, 1):
+            for way in (1, -1):
+                k = e - 1 if way == 1 else 2 + e
+                SB2[i, k, 0] = block(e * way, i).astype(BF16)
+                SB2[i, k, 1] = block((e + 4) * way, i).astype(BF16)
+                cp = rcopy(SB2.at[i, k], G.at[i, k], e2s.at[i, k], e2r.at[i, k], zdev(e * way))
+                cp.start()
+                sends.append(cp)
+
+    for i in range(2):
+        for k in (2, 5, 1, 4, 0, 3):
+            wait_bytes(G.at[i, k], e2r.at[i, k])
+        wait_bytes(G8.at[i], e8r.at[i])
+        for side, way in ((0, 1), (1, -1)):
+            total = block(4 * way, i)
+            for k in range(3):
+                total = total + G[i, 3 * side + k, 1].astype(F32)
+            if i == side:
+                total = total + G8[i].astype(F32)
+            T4[i, side] = total.astype(BF16)
+            cp = rcopy(T4.at[i, side], Fr.at[i, side], e3s.at[i, side], e3r.at[i, side], zdev(4 * way))
             cp.start()
             sends.append(cp)
-
-    for k in range(6):
-        wait_bytes(G.at[k], e2r.at[k])
-    for k in range(2):
-        wait_bytes(G8.at[k], e2r.at[6 + k])
-    for side, way in ((0, 1), (1, -1)):
-        for i in range(2):
-            total = block(4 * way, i)
-            for k in range(3):
-                total = total + G[3 * side + k, 1, i].astype(F32)
-            if i == side:
-                total = total + G8[side].astype(F32)
-            T4[side, i] = total.astype(BF16)
-        cp = rcopy(T4.at[side], Fr.at[side], e3s.at[side], e3r.at[side], zdev(4 * way))
-        cp.start()
-        sends.append(cp)
 
     totals = []
     for i in range(2):
         total = block(0, i)
         for k in range(6):
-            total = total + G[k, 0, i].astype(F32)
+            total = total + G[i, k, 0].astype(F32)
         totals.append(total)
     for cp in sends:
         cp.wait_send()
     for i in range(2):
         wait_bytes(EXs.at[i], e1s.at[i])
     wait_bytes(R.at[:, pl.ds(0, NH - 1)], dsd)
-    for side in range(2):
-        wait_bytes(Fr.at[side], e3r.at[side])
     for i in range(2):
-        total = totals[i] + Fr[0, i].astype(F32) + Fr[1, i].astype(F32)
+        for side in range(2):
+            wait_bytes(Fr.at[i, side], e3r.at[i, side])
+        total = totals[i] + Fr[i, 0].astype(F32) + Fr[i, 1].astype(F32)
         out[:, 256 * i:256 * i + 256] = total[:8].astype(BF16)
         out[:, 512 + 256 * i:768 + 256 * i] = total[8:].astype(BF16)
 
@@ -388,13 +386,14 @@
     hbm = pl.BlockSpec(memory_space=pl.ANY)
     V = pltpu.VMEM
     D = pltpu.SemaphoreType.DMA
+    operands = (tok, gw, gs, gz, uw, us, uz, sb.reshape(10, 128), dw, ds, dz)
     return pl.pallas_call(
         kernel,
         out_shape=jax.ShapeDtypeStruct((8, 1024), BF16),
-        in_specs=[vmem, hbm, vmem, vmem, hbm, vmem, vmem, vmem, hbm, vmem, vmem],
+        in_specs=[hbm] * 11,
         out_specs=vmem,
         scratch_shapes=[
-            V((256, 1280), F32), V((256, 1280), F32), V((320, 1024), F32),
+            *[V(x.shape, x.dtype) for x in operands],
             V((8, 1280), F32), V((8, 1280), F32), V((8, 1280), F32), V((8, 1280), F32),
             V((10, 1, 1024), F32), V((10, 1, 1024), F32), V((10, 1, 128), F32),
             V((10, 1024, 256), BF16),
@@ -411,17 +410,17 @@
             V((128, 1280), BF16), V((128, 1280), BF16),
             V((2, 16, 16, 256), BF16), V((2, 16, 16, 256), BF16),
             V((2, 16, 16, 256), F32),
-            V((6, 2, 2, 16, 256), BF16), V((2, 16, 256), BF16),
-            V((6, 2, 2, 16, 256), BF16), V((2, 16, 256), BF16),
+            V((2, 6, 2, 16, 256), BF16), V((2, 16, 256), BF16),
+            V((2, 6, 2, 16, 256), BF16), V((2, 16, 256), BF16),
             V((2, 2, 16, 256), BF16), V((2, 2, 16, 256), BF16),
-            D((3,)), D((8,)), D((8,)), D, D((18,)), D((2,)), D((2,)), D((2,)),
-            D((10,)), D, D, D, D, D, D((2,)), D((2,)), D((8,)), D((8,)), D((2,)), D((2,)),
+            D((11,)), D((8,)), D((8,)), D, D((18,)), D((2,)), D((2,)), D((2,)),
+            D((20,)), D, D, D, D, D, D((2,)), D((2,)), D((2, 6)), D((2, 6)), D((2,)), D((2,)), D((2, 2)), D((2, 2)),
         ],
         compiler_params=pltpu.CompilerParams(
-            collective_id=0, has_side_effects=True, vmem_limit_bytes=48 * 1024 * 1024
+            collective_id=0, has_side_effects=True, vmem_limit_bytes=60 * 1024 * 1024
         ),
         name="rotated_ffn",
-    )(tok, gw, gs, gz, uw, us, uz, sb.reshape(10, 128), dw, ds, dz)
+    )(*operands)
 
 
 def solution(mesh):

time: 99.6 us -> 83.1 us (0.83)
  local copies, waits for them, and re-layouts: 10.6 us -> 1.32 us
  Pallas kernels: 88.3 us -> 81.3 us
    unnamed x23 -> x1, local copies, waits for them, and re-layouts: 10.6 us -> 1.32 us
    pallas_call x1, Pallas kernels: 88.3 us -> 81.3 us  [body(): pl.pallas_call(kernel, out_shape=jax.ShapeDtypeStruct((8, 1024), BF16), i...]
where the time goes in v2:
time: 83.1 us; the launch traced here: 82.6 us
  Pallas kernels  81.3 us (98%)
  local copies, waits for them, and re-layouts  1.32 us (2%)
    pallas_call x1, Pallas kernels, body(): pl.pallas_call(kernel, out_shape=jax.ShapeDtypeStruct((8, 1024), BF16), i...  81.3 us

profile of v2, /device:TPU:1, one launch (start us, length us, event | category | flops | bytes accessed | tf_op | source)
XLA Modules:
  0.0 82.6 jit_solution(7706903810608470643)
XLA Ops:
  0.0 81.3 %rotated_ffn.1 = bf16[8,1024]{1,0:T(8,128)(2,1)} custom-call(bf16[8,1024]{1,0:T(8,128)(2,1)} %refs_0_.1, f32[256,1280]{1,0:T(8,128)} %refs_1_.1, bf16[8,1280]{1,0:T(8,128)(2,1)} %refs_2_.1, s32[8,1280]{1,0:T(8,128)} %refs_3_.1, f32[256,1280]{1,0:T(8,128)} %refs_4_.1, bf16[8,1280]{1,0:T(8,128)(2,1)} %refs_5_.1, s32[8,1280]{1,0:T(8,128)} %refs_6_.1, ...), custom_call_target="tpu_custom_call" | custom-call | tf_op jit(solution)/shard_map/rotated_ffn/pallas_call | solution.py:390
  81.3 1.3 %copy.13 = bf16[8,1024]{1,0:T(8,128)(2,1)} copy(bf16[8,1024]{1,0:T(8,128)(2,1)} %rotated_ffn.1) | data formatting | bytes 32768

commit v3 on v2

--- a/solution.py
+++ b/solution.py
@@ -83,6 +83,14 @@
     cols = lax.broadcasted_iota(jnp.int32, (128, 128), 1)
     place = 32 * jnp.bitwise_and(rows, 3) + jnp.right_shift(rows, 2)
     shuffle = jnp.where(place == cols, 1.0, 0.0).astype(BF16)
+    def dequant_gu(b):
+        at = pl.ds(pl.multiple_of(b * 128, 128), 128)
+        for words, zf, sf, lane in ((gw, gzf, gsf, 0), (uw, uzf, usf, 128)):
+            for g in range(8):
+                planes = dequantized(words[32 * g:32 * g + 32, at], zf[g:g + 1, at], sf[g:g + 1, at])
+                for k in range(4):
+                    W[b, 128 * g + 32 * k:128 * g + 32 * k + 32, lane:lane + 128] = planes[k]
+
     loads[0].wait()
     for g in range(4):
         both = [
@@ -91,31 +99,6 @@
         ]
         X[3, c, g] = jnp.concatenate(both, axis=0).astype(BF16)
 
-    pl.semaphore_wait(bar, len(near) + 1 + NH - 1)
-
-    stage1 = [
-        rcopy(X.at[3, c], X.at[slot_of(-e), c], as1.at[k], ar.at[slot_of(-e)], zdev(e))
-        for k, e in enumerate(near)
-    ]
-    for cp in stage1:
-        cp.start()
-
-    def to_core(s):
-        return rcopy(X.at[s, c], X.at[s, c], asc, arc.at[s // 8], other)
-
-    to_core(3).start()
-
-    def arrived(s):
-        wait_bytes(X.at[s, c], ar.at[s])
-
-    def dequant_gu(b):
-        at = pl.ds(pl.multiple_of(b * 128, 128), 128)
-        for words, zf, sf, lane in ((gw, gzf, gsf, 0), (uw, uzf, usf, 128)):
-            for g in range(8):
-                planes = dequantized(words[32 * g:32 * g + 32, at], zf[g:g + 1, at], sf[g:g + 1, at])
-                for k in range(4):
-                    W[b, 128 * g + 32 * k:128 * g + 32 * k + 32, lane:lane + 128] = planes[k]
-
     for i in (1, 2, 3, 4, 5, 6):
         loads[i].wait()
     gsf[...] = gs[...].astype(F32)
@@ -124,22 +107,22 @@
     uzf[...] = uz[...].astype(F32)
     loop(0, NB, dequant_gu)
 
-    for i in (7, 8, 9, 10):
-        loads[i].wait()
-    dsv, dzv, sgv = ds[...].astype(F32), dz[...].astype(F32), (1 - 2 * sb[...]).astype(F32)
-    for b in range(NB):
-        dsf[b], dzf[b], sgn[b] = dsv[b:b + 1], dzv[b:b + 1], sgv[b:b + 1]
-
-    def dequant_d(b):
-        at = pl.ds(pl.multiple_of(b * 32, 32), 32)
-        for q in range(8):
-            lanes = slice(128 * q, 128 * q + 128)
-            planes = dequantized(dw[at, lanes], dzf[b, :, lanes], dsf[b, :, lanes])
-            for k in range(4):
-                to = pl.ds(pl.multiple_of(b * 128 + 32 * k, 32), 32)
-                Wd[q // 2, to, 128 * (q % 2):128 * (q % 2) + 128] = planes[k]
-
-    loop(0, NB, dequant_d)
+    pl.semaphore_wait(bar, len(near) + 1 + NH - 1)
+
+    stage1 = [
+        rcopy(X.at[3, c], X.at[slot_of(-e), c], as1.at[k], ar.at[slot_of(-e)], zdev(e))
+        for k, e in enumerate(near)
+    ]
+    for cp in stage1:
+        cp.start()
+
+    def to_core(s):
+        return rcopy(X.at[s, c], X.at[s, c], asc, arc.at[s], other)
+
+    to_core(3).start()
+
+    def arrived(s):
+        wait_bytes(X.at[s, c], ar.at[s])
 
     stage2 = []
     for way in (1, -1):
@@ -160,46 +143,63 @@
         to_core(slot_of(e)).start()
     to_core(slot_of(-4)).start()
 
-    for part in range(2):
-        if part == 1:
-            for e in (5, -5, 6, -6, 7, -7):
-                arrived(slot_of(e))
-                to_core(slot_of(e)).start()
-            for half in range(2):
-                wait_bytes(X.at[slot_of(8), c, pl.ds(2 * half, 2)], ar.at[16 + half])
-            to_core(slot_of(8)).start()
-        wait_bytes(X.at[pl.ds(8 * part, 8), oc], arc.at[part])
-
-        def lay(s, part=part):
-            at = pl.ds(pl.multiple_of(16 * s, 16), 16)
+    def products(slots):
+        for s in slots:
+            wait_bytes(X.at[s, oc], arc.at[s])
+        for i, s in enumerate(slots):
             for g in range(4):
-                t0 = X[8 * part + s, 0, g].astype(F32)
-                t1 = X[8 * part + s, 1, g].astype(F32)
+                t0, t1 = X[s, 0, g].astype(F32), X[s, 1, g].astype(F32)
+                at = slice(16 * i, 16 * i + 16)
                 L[at, 128 * g:128 * g + 128] = jnp.concatenate([t0[:8], t1[:8]], axis=0).astype(BF16)
                 L[at, 512 + 128 * g:640 + 128 * g] = jnp.concatenate([t0[8:], t1[8:]], axis=0).astype(BF16)
 
-        loop(0, 8, lay)
-
-        def product(b, part=part):
-            v = jnp.dot(L[...], W[b], preferred_element_type=F32).astype(BF16)
-            for s in range(8):
-                r = 10 * s + b
+        def product(b):
+            v = jnp.dot(L[:16 * len(slots)], W[b], preferred_element_type=F32).astype(BF16)
+            for i, s in enumerate(slots):
+                n = 10 * lax.rem(z + 13 + s, 16) + b
+                m, to = lax.div(n, 16), lax.rem(n, 16)
                 for u in range(2):
-                    S[part, lax.div(r, 16), lax.rem(r, 16), u] = v[16 * s:16 * s + 16, 128 * u:128 * u + 128]
+                    S[s, b, u] = v[16 * i:16 * i + 16, 128 * u:128 * u + 128]
+
+                @pl.when(to != h)
+                def _(s=s, m=m, to=to):
+                    rcopy(S.at[s, b], B.at[m, h], bs, br.at[m], (to, j)).start()
+
+                @pl.when(to == h)
+                def _(s=s, m=m):
+                    B[m, h] = S[s, b]
 
         loop(0, NB, product)
 
-        n0 = 10 * lax.rem(z + 13 + 8 * part, 16)
-
-        def send(p, part=part, n0=n0):
-            y = lax.rem(lax.div(h, 4) + lax.div(p, 4), 4)
-            x = lax.rem(lax.rem(h, 4) + lax.rem(p, 4), 4)
-            to = 4 * y + x
-            r0 = lax.rem(to - n0 + 160, 16)
-            rcopy(S.at[part, :, r0], B.at[part, h], bs.at[part], br.at[part], (to, j)).start()
-
-        loop(1, NH, send)
-        B[part, h] = S[part, :, lax.rem(h - n0 + 160, 16)]
+    products(range(8))
+    for e in (5, -5, 6):
+        arrived(slot_of(e))
+        to_core(slot_of(e)).start()
+    products((8, 9, 14, 15))
+    for e in (-6, 7, -7):
+        arrived(slot_of(e))
+        to_core(slot_of(e)).start()
+    for half in range(2):
+        wait_bytes(X.at[slot_of(8), c, pl.ds(2 * half, 2)], ar.at[16 + half])
+    to_core(slot_of(8)).start()
+    products((10, 11, 12, 13))
+
+    for i in (7, 8, 9, 10):
+        loads[i].wait()
+    dsv, dzv, sgv = ds[...].astype(F32), dz[...].astype(F32), (1 - 2 * sb[...]).astype(F32)
+    for b in range(NB):
+        dsf[b], dzf[b], sgn[b] = dsv[b:b + 1], dzv[b:b + 1], sgv[b:b + 1]
+
+    def dequant_d(b):
+        at = pl.ds(pl.multiple_of(b * 32, 32), 32)
+        for q in range(8):
+            lanes = slice(128 * q, 128 * q + 128)
+            planes = dequantized(dw[at, lanes], dzf[b, :, lanes], dsf[b, :, lanes])
+            for k in range(4):
+                to = pl.ds(pl.multiple_of(b * 128 + 32 * k, 32), 32)
+                Wd[q // 2, to, 128 * (q % 2):128 * (q % 2) + 128] = planes[k]
+
+    loop(0, NB, dequant_d)
 
     for cp in stage1 + stage2:
         cp.wait_send()
@@ -220,23 +220,23 @@
             def _():
                 C1[j] = U[m]
 
-    for part in range(2):
-        wait_bytes(B.at[part, pl.ds(0, NH - 1)], br.at[part])
-        n0 = 10 * lax.rem(z + 13 + 8 * part, 16)
-        r0 = lax.rem(h - n0 + 160, 16)
-
-        def unit(q, part=part, n0=n0, r0=r0):
-            n = lax.rem(n0 + r0 + 16 * q, 160)
-            total = B[part, 0, q].astype(F32)
-            for s in range(1, NH):
-                total = total + B[part, s, q].astype(F32)
-            gate, up = total[0], total[1]
-            hidden = gate / (1.0 + jnp.exp(-gate)) * up
-            m = lax.div(n, 16)
-            U[m] = (hidden * sgn[lax.rem(n, 10)]).astype(BF16)
-            collect(m)
-
-        loop(0, 5, unit)
+    n0 = 10 * lax.rem(z + 13, 16)
+    n0 = n0 + lax.rem(h - n0 + 160, 16)
+
+    def unit(k):
+        n = lax.rem(n0 + 16 * k, 160)
+        m = lax.div(n, 16)
+        wait_bytes(B.at[m, pl.ds(0, NH - 1)], br.at[m])
+        total = B[m, 0].astype(F32)
+        for s in range(1, NH):
+            total = total + B[m, s].astype(F32)
+        gate, up = total[0], total[1]
+        hidden = gate / (1.0 + jnp.exp(-gate)) * up
+        U[m] = (hidden * sgn[lax.rem(n, 10)]).astype(BF16)
+        collect(m)
+
+    loop(0, 5, unit)
+    loop(0, 5, lambda i: unit(5 + (4 * lax.rem(i, 2)) + lax.div(i, 2) * (1 - 2 * lax.rem(i, 2))))
 
     owns = lax.rem(j, 8) < 5
     mine = 5 * lax.div(lax.rem(j, 16), 8) + lax.rem(j, 8)
@@ -265,27 +265,28 @@
 
             @pl.when(i != j)
             def _():
-                rcopy(C2.at[i], R2.at[mine], c2s, c2r, (h, i)).start()
+                rcopy(C2.at[i], R2.at[mine], c2s, c2r.at[mine], (h, i)).start()
 
         loop(0, 16, back)
         R2[mine] = C2[j]
-        wait_bytes(R2.at[pl.ds(0, NB - 1)], c2r)
-
-    @pl.when(jnp.logical_not(owns))
-    def _():
-        wait_bytes(R2.at[pl.ds(0, NB)], c2r)
-
-    def spread(p):
-        y = lax.rem(lax.div(h, 4) + lax.div(p, 4), 4)
-        x = lax.rem(lax.rem(h, 4) + lax.rem(p, 4), 4)
-        rcopy(R2, R.at[:, h], dsd, drv, (4 * y + x, j)).start()
-
-    loop(1, NH, spread)
-    for m in range(NB):
+
+    start = lax.div(5 * lax.rem(z, 8) + 2, 4)
+    for step in (0, 1, 9, 2, 8, 3, 7, 4, 6, 5):
+        m = lax.rem(start + step, NB)
+
+        @pl.when(jnp.logical_not(jnp.logical_and(owns, m == mine)))
+        def _(m=m):
+            wait_bytes(R2.at[m], c2r.at[m])
+
+        def spread(p, m=m):
+            y = lax.rem(lax.div(h, 4) + lax.div(p, 4), 4)
+            x = lax.rem(lax.rem(h, 4) + lax.rem(p, 4), 4)
+            rcopy(R2.at[m], R.at[m, h], dsd, drv, (4 * y + x, j)).start()
+
+        loop(1, NH, spread)
         R[m, h] = R2[m]
 
-    for part in range(2):
-        wait_bytes(S.at[part, :, pl.ds(0, NH - 1)], bs.at[part])
+    wait_bytes(S.at[pl.ds(0, 15)], bs)
 
     def collected(m):
         for side in range(2):
@@ -400,8 +401,8 @@
             V((4, 1280, 256), BF16),
             V((16, 2, 4, 16, 128), BF16),
             V((128, 1024), BF16),
-            V((2, 5, 16, 2, 16, 128), BF16),
-            V((2, 16, 5, 2, 16, 128), BF16),
+            V((16, 10, 2, 16, 128), BF16),
+            V((10, 16, 2, 16, 128), BF16),
             V((10, 16, 128), BF16),
             V((32, 16, 128), BF16),
             V((32, 16, 128), BF16),
@@ -413,8 +414,8 @@
             V((2, 6, 2, 16, 256), BF16), V((2, 16, 256), BF16),
             V((2, 6, 2, 16, 256), BF16), V((2, 16, 256), BF16),
             V((2, 2, 16, 256), BF16), V((2, 2, 16, 256), BF16),
-            D((11,)), D((8,)), D((8,)), D, D((18,)), D((2,)), D((2,)), D((2,)),
-            D((20,)), D, D, D, D, D, D((2,)), D((2,)), D((2, 6)), D((2, 6)), D((2,)), D((2,)), D((2, 2)), D((2, 2)),
+            D((11,)), D((8,)), D((8,)), D, D((18,)), D((16,)), D, D((10,)),
+            D((20,)), D, D, D((10,)), D, D, D((2,)), D((2,)), D((2, 6)), D((2, 6)), D((2,)), D((2,)), D((2, 2)), D((2, 2)),
         ],
         compiler_params=pltpu.CompilerParams(
             collective_id=0, has_side_effects=True, vmem_limit_bytes=60 * 1024 * 1024

time: 83.1 us -> 78.5 us (0.945)
  Pallas kernels: 81.3 us -> 76.9 us
    pallas_call x1, Pallas kernels: 81.3 us -> 76.9 us  [body(): pl.pallas_call(kernel, out_shape=jax.ShapeDtypeStruct((8, 1024), BF16), i...]
where the time goes in v3:
time: 78.5 us; the launch traced here: 78.2 us
  Pallas kernels  76.9 us (98%)
  local copies, waits for them, and re-layouts  1.32 us (2%)
    pallas_call x1, Pallas kernels, body(): pl.pallas_call(kernel, out_shape=jax.ShapeDtypeStruct((8, 1024), BF16), i...  76.9 us

profile of v3, /device:TPU:1, one launch (start us, length us, event | category | flops | bytes accessed | tf_op | source)
XLA Modules:
  0.0 78.2 jit_solution(5659496833159749325)
XLA Ops:
  0.0 76.9 %rotated_ffn.1 = bf16[8,1024]{1,0:T(8,128)(2,1)} custom-call(bf16[8,1024]{1,0:T(8,128)(2,1)} %refs_0_.1, f32[256,1280]{1,0:T(8,128)} %refs_1_.1, bf16[8,1280]{1,0:T(8,128)(2,1)} %refs_2_.1, s32[8,1280]{1,0:T(8,128)} %refs_3_.1, f32[256,1280]{1,0:T(8,128)} %refs_4_.1, bf16[8,1280]{1,0:T(8,128)(2,1)} %refs_5_.1, s32[8,1280]{1,0:T(8,128)} %refs_6_.1, ...), custom_call_target="tpu_custom_call" | custom-call | tf_op jit(solution)/shard_map/rotated_ffn/pallas_call | solution.py:391
  76.9 1.3 %copy.13 = bf16[8,1024]{1,0:T(8,128)(2,1)} copy(bf16[8,1024]{1,0:T(8,128)(2,1)} %rotated_ffn.1) | data formatting | bytes 32768

commit v4 on v3

--- a/solution.py
+++ b/solution.py
@@ -48,8 +48,8 @@
     tok, gw, gs, gz, uw, us, uz, sb, dw, ds, dz = held
     (
     gsf, gzf, usf, uzf, dsf, dzf, sgn,
-    W, Wd, X, L, S, B, U, C1, C2, R2, R, Lown, Loth, EXs, EXr, Pown, SB2, SB8, G, G8, T4, Fr,
-    w_sem, as1, as2, asc, ar, arc, bs, br, c1s, c1r, c2s, c2r, dsd, drv, e1s, e1r, e2s, e2r, e8s, e8r, e3s, e3r,
+    W, Wd, X, L, S, B, U, C1, C2, R2, R, Lh, EXs, EXr, Pown, SB, G, T4, Fr,
+    w_sem, as1, as2, asc, ar, arc, bs, br, c1s, c1r, c2s, c2r, dsd, drv, e1s, e1r, e2s, e2r, e3s, e3r,
     ) = scratch[11:]
     h = lax.axis_index("hid")
     j = lax.axis_index("inter")
@@ -67,7 +67,7 @@
             src_ref=src, dst_ref=dst, send_sem=ss, recv_sem=rs, device_id=dev, device_id_type=MESH
         )
 
-    near = (4, -4, 1, -1, 2, -2, 3, -3)
+    near = (4, -4, 3, -3, 2, -2, 1, -1)
     bar = pltpu.get_barrier_semaphore()
     for d in near:
         pl.semaphore_signal(bar, inc=1, device_id=zdev(d), device_id_type=MESH)
@@ -128,13 +128,13 @@
     for way in (1, -1):
         s = slot_of(-4 * way)
         arrived(s)
-        for e in (1, 2, 3):
-            to = slot_of(-(4 + e) * way)
-            stage2.append(rcopy(X.at[s, c], X.at[to, c], as2.at[len(stage2)], ar.at[to], zdev(e * way)))
         half = 0 if way == 1 else 1
         stage2.append(rcopy(
             X.at[s, c, pl.ds(2 * half, 2)], X.at[slot_of(8), c, pl.ds(2 * half, 2)],
             as2.at[len(stage2)], ar.at[16 + half], zdev(4 * way)))
+        for e in (3, 2, 1):
+            to = slot_of(-(4 + e) * way)
+            stage2.append(rcopy(X.at[s, c], X.at[to, c], as2.at[len(stage2)], ar.at[to], zdev(e * way)))
         for cp in stage2[-4:]:
             cp.start()
     to_core(slot_of(4)).start()
@@ -169,19 +169,19 @@
                 def _(s=s, m=m):
                     B[m, h] = S[s, b]
 
-        loop(0, NB, product)
+        loop(0, NB, lambda i: product(lax.rem(i + h, NB)))
 
     products(range(8))
     for e in (5, -5, 6):
         arrived(slot_of(e))
         to_core(slot_of(e)).start()
-    products((8, 9, 14, 15))
     for e in (-6, 7, -7):
         arrived(slot_of(e))
         to_core(slot_of(e)).start()
     for half in range(2):
         wait_bytes(X.at[slot_of(8), c, pl.ds(2 * half, 2)], ar.at[16 + half])
     to_core(slot_of(8)).start()
+    products((8, 9, 14, 15))
     products((10, 11, 12, 13))
 
     for i in (7, 8, 9, 10):
@@ -261,7 +261,9 @@
             C2[i] = (vals[i] * (1.0 / 64.0)).astype(BF16)
 
         def back(q):
-            i = 2 * lax.rem(z + lax.div(q, 2) + 12, 16) + lax.rem(q, 2)
+            d = lax.div(q + 2, 4)
+            d = jnp.where(lax.rem(lax.div(q, 2), 2) == 0, d - 4, 4 - d)
+            i = 2 * lax.rem(z + d + 16, 16) + lax.rem(q, 2)
 
             @pl.when(i != j)
             def _():
@@ -270,20 +272,23 @@
         loop(0, 16, back)
         R2[mine] = C2[j]
 
-    start = lax.div(5 * lax.rem(z, 8) + 2, 4)
-    for step in (0, 1, 9, 2, 8, 3, 7, 4, 6, 5):
-        m = lax.rem(start + step, NB)
+    first_half = lax.rem(lax.div(z + 1, 4), 2)
+    rising = lax.rem(z + 1, 4) < 2
+    for step in range(NB):
+        half = first_half if step < 5 else 1 - first_half
+        m = 5 * half + jnp.where(rising, step % 5, 4 - step % 5)
 
         @pl.when(jnp.logical_not(jnp.logical_and(owns, m == mine)))
         def _(m=m):
             wait_bytes(R2.at[m], c2r.at[m])
 
-        def spread(p, m=m):
-            y = lax.rem(lax.div(h, 4) + lax.div(p, 4), 4)
-            x = lax.rem(lax.rem(h, 4) + lax.rem(p, 4), 4)
-            rcopy(R2.at[m], R.at[m, h], dsd, drv, (4 * y + x, j)).start()
-
-        loop(1, NH, spread)
+        def spread(p, m=m, half=half):
+            y = lax.rem(lax.div(h, 4) + lax.div(p + 10, 4), 4)
+            x = lax.rem(h + p + 10, 4)
+            rcopy(R2.at[m], R.at[m, h], dsd, drv.at[half], (4 * y + x, j)).start()
+
+        loop(0, 6, spread)
+        loop(7, NH, spread)
         R[m, h] = R2[m]
 
     wait_bytes(S.at[pl.ds(0, 15)], bs)
@@ -300,64 +305,66 @@
     def _():
         wait_bytes(C2.at[pl.ds(0, 15)], c2s)
 
-    wait_bytes(R.at[:, pl.ds(0, NH - 1)], drv)
-
-    def split(a):
-        at = pl.ds(pl.multiple_of(16 * a, 16), 16)
-        for b in range(NB):
-            n = 20 * a + b
-            t0 = R[lax.div(n, 16), lax.rem(n, 16)].astype(F32)
-            t1 = R[lax.div(n + 10, 16), lax.rem(n + 10, 16)].astype(F32)
-            low = jnp.concatenate([t0[:8], t1[:8]], axis=0)
-            high = jnp.concatenate([t0[8:], t1[8:]], axis=0)
-            lanes = slice(128 * b, 128 * b + 128)
-            Lown[at, lanes] = jnp.where(c == 0, low, high).astype(BF16)
-            Loth[at, lanes] = jnp.where(c == 0, high, low).astype(BF16)
-
-    loop(0, 8, split)
-
-    def pair(lhs, i):
-        lo = jnp.dot(lhs[...], Wd[i], preferred_element_type=F32).reshape(NZ, 8, 256)
-        hi = jnp.dot(lhs[...], Wd[2 + i], preferred_element_type=F32).reshape(NZ, 8, 256)
-        return jnp.concatenate([lo, hi], axis=1)
-
-    def for_other(i):
-        EXs[i] = pair(Loth, i).astype(BF16)
-        rcopy(EXs.at[i], EXr.at[i], e1s.at[i], e1r.at[i], other).start()
-
-    loop(0, 2, for_other)
-
-    def block(d, i):
-        at = lax.rem(z + d + 16, 16)
+    def block(at, i):
         return Pown[i, at] + EXr[i, at].astype(F32)
+
+    def chip_at(d):
+        return lax.rem(z + d + 16, 16)
+
+    for half in (first_half, 1 - first_half):
+        wait_bytes(R.at[pl.ds(5 * half, 5), pl.ds(0, NH - 1)], drv.at[half])
+
+        def split(a, half=half):
+            for b in range(NB):
+                n = 80 * half + 20 * a + b
+                t0 = R[lax.div(n, 16), lax.rem(n, 16)].astype(F32)
+                t1 = R[lax.div(n + 10, 16), lax.rem(n + 10, 16)].astype(F32)
+                low = jnp.concatenate([t0[:8], t1[:8]], axis=0)
+                high = jnp.concatenate([t0[8:], t1[8:]], axis=0)
+                lanes = slice(128 * b, 128 * b + 128)
+                at = pl.multiple_of(16 * a, 16)
+                Lh[pl.ds(at, 16), lanes] = jnp.where(c == 0, high, low).astype(BF16)
+                Lh[pl.ds(at + 64, 16), lanes] = jnp.where(c == 0, low, high).astype(BF16)
+
+        loop(0, 4, split)
+
+        def exchange(i, half=half):
+            lo = jnp.dot(Lh[...], Wd[i], preferred_element_type=F32).reshape(16, 8, 256)
+            hi = jnp.dot(Lh[...], Wd[2 + i], preferred_element_type=F32).reshape(16, 8, 256)
+            both = jnp.concatenate([lo, hi], axis=1)
+            eight = pl.ds(8 * half, 8)
+            EXs[i, eight] = both[:8].astype(BF16)
+            rcopy(EXs.at[i, eight], EXr.at[i, eight], e1s.at[half, i], e1r.at[half, i], other).start()
+            Pown[i, eight] = both[8:]
+
+        loop(0, 2, exchange)
+
+        for i in range(2):
+            wait_bytes(EXr.at[i, pl.ds(8 * half, 8)], e1r.at[half, i])
+
+            def outward(q, half=half, i=i):
+                at = 8 * half + q
+                d = lax.rem(at - z + 16, 16)
+                to = jnp.where(d < 4, d, jnp.where(d < 8, d - 4, jnp.where(d < 12, d + 4, d)))
+                to = jnp.where(d == 8, 4 if i == 0 else 12, to)
+
+                @pl.when(jnp.logical_or(lax.rem(d, 4) != 0, d == 8))
+                def _():
+                    SB[i, d] = block(at, i).astype(BF16)
+                    rcopy(SB.at[i, d], G.at[i, d], e2s.at[i], e2r.at[i, d], zdev(to)).start()
+
+            loop(0, 8, outward)
 
     sends = []
     for i in range(2):
-        Pown[i] = pair(Lown, i)
-        wait_bytes(EXr.at[i], e1r.at[i])
-        SB8[i] = block(8, i).astype(BF16)
-        cp = rcopy(SB8.at[i], G8.at[i], e8s.at[i], e8r.at[i], zdev(4 if i == 0 else -4))
-        cp.start()
-        sends.append(cp)
-        for e in (3, 2, 1):
-            for way in (1, -1):
-                k = e - 1 if way == 1 else 2 + e
-                SB2[i, k, 0] = block(e * way, i).astype(BF16)
-                SB2[i, k, 1] = block((e + 4) * way, i).astype(BF16)
-                cp = rcopy(SB2.at[i, k], G.at[i, k], e2s.at[i, k], e2r.at[i, k], zdev(e * way))
-                cp.start()
-                sends.append(cp)
-
-    for i in range(2):
-        for k in (2, 5, 1, 4, 0, 3):
-            wait_bytes(G.at[i, k], e2r.at[i, k])
-        wait_bytes(G8.at[i], e8r.at[i])
+        for d in (8, 7, 9, 6, 10, 5, 11):
+            wait_bytes(G.at[i, d], e2r.at[i, d])
         for side, way in ((0, 1), (1, -1)):
-            total = block(4 * way, i)
-            for k in range(3):
-                total = total + G[i, 3 * side + k, 1].astype(F32)
+            total = block(chip_at(4 * way), i)
+            for d in ((5, 6, 7), (9, 10, 11))[side]:
+                total = total + G[i, d].astype(F32)
             if i == side:
-                total = total + G8[i].astype(F32)
+                total = total + G[i, 8].astype(F32)
             T4[i, side] = total.astype(BF16)
             cp = rcopy(T4.at[i, side], Fr.at[i, side], e3s.at[i, side], e3r.at[i, side], zdev(4 * way))
             cp.start()
@@ -365,14 +372,17 @@
 
     totals = []
     for i in range(2):
-        total = block(0, i)
-        for k in range(6):
-            total = total + G[i, k, 0].astype(F32)
+        total = block(z, i)
+        for d in (1, 2, 3, 13, 14, 15):
+            wait_bytes(G.at[i, d], e2r.at[i, d])
+            total = total + G[i, d].astype(F32)
         totals.append(total)
     for cp in sends:
         cp.wait_send()
     for i in range(2):
-        wait_bytes(EXs.at[i], e1s.at[i])
+        wait_bytes(G.at[i, pl.ds(0, 13)], e2s.at[i])
+        for half in range(2):
+            wait_bytes(EXs.at[i, pl.ds(8 * half, 8)], e1s.at[half, i])
     wait_bytes(R.at[:, pl.ds(0, NH - 1)], dsd)
     for i in range(2):
         for side in range(2):
@@ -408,14 +418,13 @@
             V((32, 16, 128), BF16),
             V((10, 16, 128), BF16),
             V((10, 16, 16, 128), BF16),
-            V((128, 1280), BF16), V((128, 1280), BF16),
+            V((128, 1280), BF16),
             V((2, 16, 16, 256), BF16), V((2, 16, 16, 256), BF16),
             V((2, 16, 16, 256), F32),
-            V((2, 6, 2, 16, 256), BF16), V((2, 16, 256), BF16),
-            V((2, 6, 2, 16, 256), BF16), V((2, 16, 256), BF16),
+            V((2, 16, 16, 256), BF16), V((2, 16, 16, 256), BF16),
             V((2, 2, 16, 256), BF16), V((2, 2, 16, 256), BF16),
             D((11,)), D((8,)), D((8,)), D, D((18,)), D((16,)), D, D((10,)),
-            D((20,)), D, D, D((10,)), D, D, D((2,)), D((2,)), D((2, 6)), D((2, 6)), D((2,)), D((2,)), D((2, 2)), D((2, 2)),
+            D((20,)), D, D, D((10,)), D, D((2,)), D((2, 2)), D((2, 2)), D((2,)), D((2, 16)), D((2, 2)), D((2, 2)),
         ],
         compiler_params=pltpu.CompilerParams(
             collective_id=0, has_side_effects=True, vmem_limit_bytes=60 * 1024 * 1024

time: 78.5 us -> 76.5 us (0.975)
  Pallas kernels: 76.9 us -> 74.9 us
    pallas_call x1, Pallas kernels: 76.9 us -> 74.9 us  [body(): pl.pallas_call(kernel, out_shape=jax.ShapeDtypeStruct((8, 1024), BF16), i...]
where the time goes in v4:
time: 76.5 us; the launch traced here: 76.2 us
  Pallas kernels  74.9 us (98%)
  local copies, waits for them, and re-layouts  1.32 us (2%)
    pallas_call x1, Pallas kernels, body(): pl.pallas_call(kernel, out_shape=jax.ShapeDtypeStruct((8, 1024), BF16), i...  74.9 us

profile of v4, /device:TPU:1, one launch (start us, length us, event | category | flops | bytes accessed | tf_op | source)
XLA Modules:
  0.0 76.2 jit_solution(4329269250709575401)
XLA Ops:
  0.0 74.9 %rotated_ffn.1 = bf16[8,1024]{1,0:T(8,128)(2,1)} custom-call(bf16[8,1024]{1,0:T(8,128)(2,1)} %refs_0_.1, f32[256,1280]{1,0:T(8,128)} %refs_1_.1, bf16[8,1280]{1,0:T(8,128)(2,1)} %refs_2_.1, s32[8,1280]{1,0:T(8,128)} %refs_3_.1, f32[256,1280]{1,0:T(8,128)} %refs_4_.1, bf16[8,1280]{1,0:T(8,128)(2,1)} %refs_5_.1, s32[8,1280]{1,0:T(8,128)} %refs_6_.1, ...), custom_call_target="tpu_custom_call" | custom-call | tf_op jit(solution)/shard_map/rotated_ffn/pallas_call | solution.py:401
  74.9 1.3 %copy.13 = bf16[8,1024]{1,0:T(8,128)(2,1)} copy(bf16[8,1024]{1,0:T(8,128)(2,1)} %rotated_ffn.1) | data formatting | bytes 32768

commit v5 on v4

--- a/solution.py
+++ b/solution.py
@@ -105,7 +105,7 @@
     usf[...] = us[...].astype(F32)
     gzf[...] = gz[...].astype(F32)
     uzf[...] = uz[...].astype(F32)
-    loop(0, NB, dequant_gu)
+    loop(0, 4, dequant_gu)
 
     pl.semaphore_wait(bar, len(near) + 1 + NH - 1)
 
@@ -120,6 +120,7 @@
         return rcopy(X.at[s, c], X.at[s, c], asc, arc.at[s], other)
 
     to_core(3).start()
+    loop(4, NB, dequant_gu)
 
     def arrived(s):
         wait_bytes(X.at[s, c], ar.at[s])

time: 76.5 us -> 75.4 us (0.986)
  Pallas kernels: 74.9 us -> 73.8 us
    pallas_call x1, Pallas kernels: 74.9 us -> 73.8 us  [body(): pl.pallas_call(kernel, out_shape=jax.ShapeDtypeStruct((8, 1024), BF16), i...]
where the time goes in v5:
time: 75.4 us; the launch traced here: 75.1 us
  Pallas kernels  73.8 us (98%)
  local copies, waits for them, and re-layouts  1.32 us (2%)
    pallas_call x1, Pallas kernels, body(): pl.pallas_call(kernel, out_shape=jax.ShapeDtypeStruct((8, 1024), BF16), i...  73.8 us

profile of v5, /device:TPU:1, one launch (start us, length us, event | category | flops | bytes accessed | tf_op | source)
XLA Modules:
  0.0 75.1 jit_solution(16193862204966600079)
XLA Ops:
  0.0 73.8 %rotated_ffn.1 = bf16[8,1024]{1,0:T(8,128)(2,1)} custom-call(bf16[8,1024]{1,0:T(8,128)(2,1)} %refs_0_.1, f32[256,1280]{1,0:T(8,128)} %refs_1_.1, bf16[8,1280]{1,0:T(8,128)(2,1)} %refs_2_.1, s32[8,1280]{1,0:T(8,128)} %refs_3_.1, f32[256,1280]{1,0:T(8,128)} %refs_4_.1, bf16[8,1280]{1,0:T(8,128)(2,1)} %refs_5_.1, s32[8,1280]{1,0:T(8,128)} %refs_6_.1, ...), custom_call_target="tpu_custom_call" | custom-call | tf_op jit(solution)/shard_map/rotated_ffn/pallas_call | solution.py:402
  73.8 1.3 %copy.13 = bf16[8,1024]{1,0:T(8,128)(2,1)} copy(bf16[8,1024]{1,0:T(8,128)(2,1)} %rotated_ffn.1) | data formatting | bytes 32768
